TPU v7x, 128 devices: a whole 4x4x4 slice. The times are simulated.
128 devices in a mesh: dom: 8 (over y, core), slab: 16 (over z, x).
Axes of the slice: x: 4, y: 4, z: 4, core: 2. Of those that a mesh axis runs over, the one named last changes fastest.
Arguments:
- heat_level: float32 [2097152], P(('dom', 'slab')), may hold values from -6 to 6
- emitting_vertex_position: int32 [128, 3, 3, 8192], P(('dom', 'slab')), may hold values from 0 to 16383
- corner_holder_shift: int32 [4, 64, 128, 512], P(None, 'dom', 'slab'), may hold values from 0 to 8, as said below
- corner_fetched_bucket: int32 [4, 64, 128, 512], P(None, 'dom', 'slab'), may hold values from 0 to 8191
- corner_factors: float32 [4, 64, 128, 512], P(None, 'dom', 'slab'), may hold values from 0.05 to 0.5
- diagonal_rigidity: float32 [64, 128, 512], P('dom', 'slab'), may hold values from 0.25 to 2
- boundary_vertex_position: int32 [128, 3, 3, 128], P(('dom', 'slab')), may hold values from 0 to 32767
- boundary_bucket_tally: int32 [128, 9], P(('dom', 'slab')), may hold values from 1 to 128, 576 in all within a row
- boundary_accepting_vertex: int32 [128, 3, 3, 128], P(('dom', 'slab')), may hold values from 0 to 16383
Outputs:
- displacement: float32 [3, 64, 128, 512], P(None, 'dom', 'slab')
- thermal_disp: float32 [3, 2097152], P(None, ('dom', 'slab'))
Inputs may be any that keep to these rules, and one draw needn't show every extreme that they name: emitting_vertex_position stays below 16384. corner_holder_shift is 3 a + b for an offset (a, b) of the hex node's device that names a device inside the mesh.
All inputs are finite; a program needn't handle non-finite values.
Results may differ from a plain program's by a relative error of at most 0.0001.
Values sent between devices are 32-bit elements; how exact they have to be, the bound alone decides.
A program may use at most 192 MiB of HBM per device.

v0:
```python
import functools
import math

import jax
import jax.numpy as jnp
from jax import lax
from jax.sharding import Mesh
from jax.sharding import PartitionSpec as P

ITERS = 4
DOM_SLAB = ("dom_0", "dom_1", "slab_0", "slab_1")
DOM = ("dom_0", "dom_1")
SLAB = ("slab_0", "slab_1")


COEF = 0.5


def with_halo(shard, sides, width):
    for axis, dim in sides:
        peers, length = (lax.axis_size(axis), shard.shape[dim])
        up = [(i, (i + 1) % peers) for i in range(peers - 1)]
        down = [(j, i) for i, j in up]
        last = lax.slice_in_dim(shard, length - width, length, axis=dim)
        leading = lax.slice_in_dim(shard, 0, width, axis=dim)
        before = lax.ppermute(last, axis, up)
        after = lax.ppermute(leading, axis, down)
        shard = jnp.concatenate([before, shard, after], axis=dim)
    return shard


def one_axis_at_a_time(shard, axes):
    return functools.reduce(lax.psum, axes, shard)


def fetch_entries(source_table, positions):
    entry_count = source_table.shape[0]
    lane_count = math.gcd(entry_count, 128)
    table_rows = source_table.reshape(entry_count // lane_count, lane_count)
    picked = table_rows[positions // lane_count]
    lane_ids = jnp.arange(lane_count, dtype=jnp.int32)
    chosen = lane_ids == (positions % lane_count)[..., None]
    return jnp.sum(jnp.where(chosen, picked, jnp.zeros_like(picked)), axis=-1)


def spread_entries(values, positions, entry_count):
    lane_count = math.gcd(entry_count, 128)
    row_count = entry_count // lane_count
    row_hot = (
        (positions // lane_count)[:, None] == jnp.arange(row_count, dtype=jnp.int32)[None, :]
    ).astype(jnp.float32)
    lane_hot = (
        (positions % lane_count)[:, None] == jnp.arange(lane_count, dtype=jnp.int32)[None, :]
    ).astype(jnp.float32)
    weighted = values[:, :, None] * lane_hot[None]
    summed = jnp.einsum("kh,ckl->chl", row_hot, weighted, precision=lax.Precision.HIGHEST)
    return summed.reshape(values.shape[0], entry_count)


def operate(bucket_entries, diagonal_rigidity, padded=None):
    if padded is None:
        padded = with_halo(bucket_entries, ((DOM, 1), (SLAB, 2)), 1)
    interior = padded[:, 1:-1, 1:-1, :]
    along_z = jnp.pad(interior, ((0, 0), (0, 0), (0, 0), (1, 1)))
    beside = padded[:, 2:, 1:-1, :] + padded[:, :-2, 1:-1, :]
    beside = beside + padded[:, 1:-1, 2:, :] + padded[:, 1:-1, :-2, :]
    beside = beside + along_z[:, :, :, 2:] + along_z[:, :, :, :-2]
    return (6.0 + diagonal_rigidity)[None] * bucket_entries - beside


def paired(residual, applied):
    return (
        one_axis_at_a_time(jnp.sum(residual * residual), DOM_SLAB),
        one_axis_at_a_time(jnp.sum(residual * applied), DOM_SLAB),
    )


def gradients(padded):
    interior = padded[1:-1, 1:-1, :]
    along_z = jnp.pad(interior, ((0, 0), (0, 0), (1, 1)))
    return COEF * jnp.stack(
        [
            padded[2:, 1:-1, :] - padded[:-2, 1:-1, :],
            padded[1:-1, 2:, :] - padded[1:-1, :-2, :],
            along_z[:, :, 2:] - along_z[:, :, :-2],
        ]
    )


def on_device(
    heat_level,
    emitting_vertex_position,
    corner_holder_shift,
    corner_fetched_bucket,
    corner_factors,
    diagonal_rigidity,
    boundary_vertex_position,
    boundary_bucket_tally,
    boundary_accepting_vertex,
):
    departing_entries = fetch_entries(heat_level, emitting_vertex_position[0])
    slots = departing_entries.shape[2]
    gathered = with_halo(departing_entries, ((DOM, 0), (SLAB, 1)), 1)
    flat_slots = gathered[::2, ::2, :].reshape(-1)
    interp = jnp.zeros(diagonal_rigidity.shape, jnp.float32)
    for corner in range(4):
        column = corner_holder_shift[corner] * slots + corner_fetched_bucket[corner]
        interp = interp + corner_factors[corner] * fetch_entries(flat_slots, column)
    first_pad = None
    dom_pos = lax.axis_index(DOM)
    slab_pos = lax.axis_index(SLAB)
    dom_count = lax.axis_size(DOM)
    slab_count = lax.axis_size(SLAB)
    deep = with_halo(interp, ((DOM, 0), (SLAB, 1)), 2)
    widened = gradients(deep)
    row_ids = jnp.arange(widened.shape[1], dtype=jnp.int32)
    col_ids = jnp.arange(widened.shape[2], dtype=jnp.int32)
    row_inside = ((row_ids > 0) | (dom_pos > 0)) & (
        (row_ids < widened.shape[1] - 1) | (dom_pos < dom_count - 1)
    )
    col_inside = ((col_ids > 0) | (slab_pos > 0)) & (
        (col_ids < widened.shape[2] - 1) | (slab_pos < slab_count - 1)
    )
    inside = row_inside[:, None] & col_inside[None, :]
    widened = jnp.where(inside[None, :, :, None], widened, jnp.zeros_like(widened))
    thermal_load = widened[:, 1:-1, 1:-1, :]
    first_pad = widened
    solution = jnp.zeros_like(thermal_load)
    residual = thermal_load
    applied = operate(residual, diagonal_rigidity, first_pad)
    norm_now, product = paired(residual, applied)
    step_size = norm_now / product
    direction = residual
    along = applied
    for iteration in range(ITERS):
        solution = solution + step_size * direction
        residual = residual - step_size * along
        if iteration + 1 < ITERS:
            applied = operate(residual, diagonal_rigidity)
            norm_next, product = paired(residual, applied)
            beta_ratio = norm_next / norm_now
            step_size = norm_next / (product - beta_ratio * norm_next / step_size)
            direction = residual + beta_ratio * direction
            along = applied + beta_ratio * along
            norm_now = norm_next
    flat_solution = solution.reshape(3, -1)
    surface_positions = boundary_vertex_position[0]
    surface_values = jnp.stack(
        [fetch_entries(flat_solution[component], surface_positions) for component in range(3)]
    )
    wslots = surface_values.shape[3]
    live_mask = (
        jnp.arange(wslots, dtype=jnp.int32)[None, None, :]
        < boundary_bucket_tally[0].reshape(3, 3)[:, :, None]
    )
    surface_values = jnp.where(live_mask[None], surface_values, jnp.zeros_like(surface_values))
    returned = with_halo(surface_values, ((DOM, 1), (SLAB, 2)), 1)
    arrived = returned[:, ::2, ::2, :]
    thermal_disp = spread_entries(
        arrived.reshape(3, -1), boundary_accepting_vertex[0].reshape(-1), heat_level.shape[0]
    )
    return (solution, thermal_disp)


def solution(mesh):
    split = Mesh(mesh.devices.reshape(4, 2, 4, 4), ("dom_0", "dom_1", "slab_0", "slab_1"))
    in_specs = (
        P(DOM_SLAB),
        P(DOM_SLAB, None, None, None),
        P(None, DOM, SLAB, None),
        P(None, DOM, SLAB, None),
        P(None, DOM, SLAB, None),
        P(DOM, SLAB, None),
        P(DOM_SLAB, None, None, None),
        P(DOM_SLAB, None),
        P(DOM_SLAB, None, None, None),
    )
    out_specs = (P(None, DOM, SLAB, None), P(None, DOM_SLAB))
    return jax.shard_map(
        on_device, mesh=split, in_specs=in_specs, out_specs=out_specs, check_vma=False
    )
```

profile of v0, /device:TPU:1, one launch (start us, length us, event | category | flops | bytes accessed | tf_op | source)
XLA Modules:
  0.0 1022.4 jit_solution(2507196898920351269)
XLA Ops:
  0.6 2.5 compare_select_fusion
  4.5 242.5 %gather_fusion = f32[73728,128]{1,0:T(8,128)} fusion(f32[128,128]{1,0:T(8,128)S(1)} %bitcast.178, s32[73728]{0:T(1024)S(1)} %broadcast_clamp_fusion), kind=kCustom, calls=%fused_computation | custom fusion | bytes 75792384 | tf_op jit(solution)/shard_map/gather | solution.py:40
  247.0 26.3 %select_reduce_fusion = f32[3,3,8192]{2,1,0:T(4,128)S(1)} fusion(f32[3,3,8192,128]{3,2,1,0:T(8,128)} %bitcast.179, s32[3,3,8192]{2,1,0:T(4,128)S(1)} %add_select_fusion), kind=kLoop, calls=%fused_computation.8 | loop fusion | flops 28237824 | bytes 38338560 | tf_op jit(solution)/shard_map/reduce_sum | solution.py:43
  273.4 4.6 collective-permute-start
  281.6 2.7 collective-permute-done.1
  284.6 3.1 collective-permute-start.2
  289.9 3.8 collective-permute-done.3
  294.2 3.4 slice.244
  297.8 108.3 %gather_fusion.2 = f32[32768,128]{1,0:T(8,128)} fusion(f32[576,128]{1,0:T(8,128)S(1)} %reshape_reshape.2, s32[32768]{0:T(1024)S(1)} %broadcast_clamp_fusion.3), kind=kCustom, calls=%fused_computation.2 | custom fusion | bytes 33685504 | tf_op jit(solution)/shard_map/gather | solution.py:40
  406.1 108.3 %gather_fusion.1 = f32[32768,128]{1,0:T(8,128)} fusion(f32[576,128]{1,0:T(8,128)S(1)} %reshape_reshape.2, s32[32768]{0:T(1024)S(1)} %broadcast_clamp_fusion.4), kind=kCustom, calls=%fused_computation.1 | custom fusion | bytes 33685504 | tf_op jit(solution)/shard_map/gather | solution.py:40
  514.4 108.2 %gather_fusion.3 = f32[32768,128]{1,0:T(8,128)} fusion(f32[576,128]{1,0:T(8,128)S(1)} %reshape_reshape.2, s32[32768]{0:T(1024)S(1)} %broadcast_clamp_fusion.2), kind=kCustom, calls=%fused_computation.3 | custom fusion | bytes 33685504 | tf_op jit(solution)/shard_map/gather | solution.py:40
  622.6 108.2 %gather_fusion.4 = f32[32768,128]{1,0:T(8,128)} fusion(f32[576,128]{1,0:T(8,128)S(1)} %reshape_reshape.2, s32[32768]{0:T(1024)S(1)} %broadcast_clamp_fusion.1), kind=kCustom, calls=%fused_computation.4 | custom fusion | bytes 33685504 | tf_op jit(solution)/shard_map/gather | solution.py:40
  730.8 22.5 %select_reduce_fusion.3 = (f32[8,8,512]{2,1,0:T(8,128)S(1)}, f32[8,8,512]{2,1,0:T(8,128)S(1)}) fusion(f32[8,8,512,128]{3,2,1,0:T(8,128)} %bitcast.182, s32[8,8,512]{2,1,0:T(8,128)S(1)} %copy-done.11, f32[8,8,512,128]{3,2,1,0:T(8,128)} %bitcast.183, s32[8,8,512]{2,1,0:T(8,128)S(1)} %copy-done.10), kind=kLoop, calls=%fused_computation.14 | loop fusion | flops 25100288 | bytes 34078720 | tf_op jit(solution)/shard_map/reduce_sum | solution.py:43
  753.4 20.8 %select_reduce_fusion.1 = (f32[8,8,512]{2,1,0:T(8,128)S(1)}, f32[8,8,512]{2,1,0:T(8,128)S(1)}) fusion(f32[8,8,512,128]{3,2,1,0:T(8,128)S(1)} %bitcast.181, s32[8,8,512]{2,1,0:T(8,128)S(1)} %copy-done.8, f32[8,8,512,128]{3,2,1,0:T(8,128)S(1)} %bitcast.180, s32[8,8,512]{2,1,0:T(8,128)S(1)} %copy-done.9), kind=kLoop, calls=%fused_computation.10 | loop fusion | flops 25100288 | bytes 34078720 | tf_op jit(solution)/shard_map/reduce_sum | solution.py:43
  775.4 4.5 collective-permute-start.4
  781.8 3.3 collective-permute-done.5
  785.1 3.1 collective-permute-start.6
  789.6 3.5 collective-permute-done.7
  794.7 8.1 all-reduce.16
  802.8 5.2 all-reduce.20
  808.0 11.3 %all-reduce.12 = (f32[]{:T(128)}, f32[]{:T(128)}) all-reduce(f32[]{:T(128)} %get-tuple-element.43, f32[]{:T(128)} %get-tuple-element.44), channel_id=1, replica_groups=mesh['dom_0'=4,'dom_1'=2,'slab_0'=4,'slab_1'=4] {'slab_0'}, use_global_device_ids=true, to_apply=%region_8.9 | all-reduce | flops 2 | bytes 16 | tf_op jit(solution)/shard_map/psum | solution.py:33
  819.3 9.1 all-reduce.8
  829.9 6.3 collective-permute-start.8
  836.2 2.3 collective-permute-start.9
  841.1 4.0 collective-permute-start.11
  847.3 6.8 all-reduce.15
  854.2 8.3 all-reduce.19
  862.4 10.0 all-reduce.11
  872.4 6.7 all-reduce.7
  884.0 6.0 collective-permute-start.12
  894.6 4.3 collective-permute-start.15
  901.1 6.8 all-reduce.14
  907.9 7.8 all-reduce.18
  915.7 12.3 %all-reduce.10 = (f32[]{:T(128)}, f32[]{:T(128)}) all-reduce(f32[]{:T(128)} %get-tuple-element.39, f32[]{:T(128)} %get-tuple-element.40), channel_id=1, replica_groups=mesh['dom_0'=4,'dom_1'=2,'slab_0'=4,'slab_1'=4] {'slab_0'}, use_global_device_ids=true, to_apply=%region_28.29 | all-reduce | flops 2 | bytes 16 | tf_op jit(solution)/shard_map/psum | solution.py:33
  928.0 6.6 all-reduce.6
  938.6 6.0 collective-permute-start.16
  949.1 4.3 collective-permute-start.19
  955.6 6.8 all-reduce.13
  962.4 8.0 all-reduce.17
  970.3 12.3 %all-reduce.9 = (f32[]{:T(128)}, f32[]{:T(128)}) all-reduce(f32[]{:T(128)} %get-tuple-element.37, f32[]{:T(128)} %get-tuple-element.38), channel_id=1, replica_groups=mesh['dom_0'=4,'dom_1'=2,'slab_0'=4,'slab_1'=4] {'slab_0'}, use_global_device_ids=true, to_apply=%region_38.39 | all-reduce | flops 2 | bytes 16 | tf_op jit(solution)/shard_map/psum | solution.py:33
  982.6 6.6 all-reduce.5
  993.4 2.4 gather_fusion.5
  995.8 2.4 gather_fusion.6
  998.3 2.4 gather_fusion.7
  1001.5 5.4 collective-permute-start.20
  1008.9 3.0 collective-permute-done.21
  1011.9 3.6 collective-permute-start.22
  1016.9 3.0 collective-permute-done.23
  (129 shorter events, 39.7 us)
Async XLA Ops:
  0.6 3.9 copy-start
  247.0 32.9 %copy-start.5 = (s32[4,8,8,512]{3,2,1,0:T(8,128)S(1)}, s32[4,8,8,512]{3,2,1,0:T(8,128)}, u32[]{:S(2)}) copy-start(s32[4,8,8,512]{3,2,1,0:T(8,128)} %param.12) | copy-start | bytes 1572868
  247.0 32.9 %copy-start.6 = (s32[4,8,8,512]{3,2,1,0:T(8,128)S(1)}, s32[4,8,8,512]{3,2,1,0:T(8,128)}, u32[]{:S(2)}) copy-start(s32[4,8,8,512]{3,2,1,0:T(8,128)} %param.11) | copy-start | bytes 1572868
  247.0 42.0 %copy-start.12 = (f32[8,8,512]{2,1,0:T(8,128)S(1)}, f32[8,8,512]{2,1,0:T(8,128)}, u32[]{:S(2)}) copy-start(f32[8,8,512]{2,1,0:T(8,128)} %param.14) | copy-start | bytes 393220
  273.4 8.2 collective-permute-start
  278.0 6.3 collective-permute-start.1
  284.6 5.4 collective-permute-start.2
  287.7 6.1 collective-permute-start.3
  622.5 108.2 %copy-start.10 = (s32[8,8,512]{2,1,0:T(8,128)S(1)}, s32[8,8,512]{2,1,0:T(8,128)}, u32[]{:S(2)}) copy-start(s32[8,8,512]{2,1,0:T(8,128)} %get-tuple-element.48) | copy-start | bytes 393220
  622.6 108.2 %copy-start.11 = (s32[8,8,512]{2,1,0:T(8,128)S(1)}, s32[8,8,512]{2,1,0:T(8,128)}, u32[]{:S(2)}) copy-start(s32[8,8,512]{2,1,0:T(8,128)} %get-tuple-element.49) | copy-start | bytes 393220
  730.8 22.5 %copy-start.2 = (f32[32768,128]{1,0:T(8,128)S(1)}, f32[32768,128]{1,0:T(8,128)}, u32[]{:S(2)}) copy-start(f32[32768,128]{1,0:T(8,128)} %gather_fusion.3) | copy-start | bytes 50331652
  730.8 22.6 %copy-start.3 = (f32[32768,128]{1,0:T(8,128)S(1)}, f32[32768,128]{1,0:T(8,128)}, u32[]{:S(2)}) copy-start(f32[32768,128]{1,0:T(8,128)} %gather_fusion.4) | copy-start | bytes 50331652
  730.8 22.6 %copy-start.8 = (s32[8,8,512]{2,1,0:T(8,128)S(1)}, s32[8,8,512]{2,1,0:T(8,128)}, u32[]{:S(2)}) copy-start(s32[8,8,512]{2,1,0:T(8,128)} %get-tuple-element.50) | copy-start | bytes 393220
  730.8 22.6 %copy-start.9 = (s32[8,8,512]{2,1,0:T(8,128)S(1)}, s32[8,8,512]{2,1,0:T(8,128)}, u32[]{:S(2)}) copy-start(s32[8,8,512]{2,1,0:T(8,128)} %get-tuple-element.51) | copy-start | bytes 393220
  753.4 40.4 %copy-start.4 = (f32[8,8,512]{2,1,0:T(8,128)S(1)}, f32[8,8,512]{2,1,0:T(8,128)}, u32[]{:S(2)}) copy-start(f32[8,8,512]{2,1,0:T(8,128)} %broadcast_add_fusion) | copy-start | bytes 393220
  753.4 138.6 %copy-start.13 = (s32[1,3,3,128]{3,0,2,1:T(1,128)S(1)}, s32[1,3,3,128]{3,0,2,1:T(1,128)}, u32[]{:S(2)}) copy-start(s32[1,3,3,128]{3,0,2,1:T(1,128)} %param.15) | copy-start | bytes 13828
  753.4 139.1 %copy-start.15 = (s32[1,9]{1,0:T(1,128)S(1)}, s32[1,9]{1,0:T(1,128)}, u32[]{:S(2)}) copy-start(s32[1,9]{1,0:T(1,128)} %param.16) | copy-start | bytes 112
  775.4 6.4 collective-permute-start.4
  779.8 5.2 collective-permute-start.5
  785.1 4.5 collective-permute-start.6
  788.2 4.8 collective-permute-start.7
  829.7 192.6 %copy-start.1 = (f32[16384]{0:T(1024)S(1)}, f32[16384]{0:T(1024)}, u32[]{:S(2)}) copy-start(f32[16384]{0:T(1024)} %param.9) | copy-start | bytes 196612
  829.9 8.6 collective-permute-start.8
  836.2 3.5 collective-permute-start.9
  839.8 5.7 collective-permute-start.10
  841.1 5.3 collective-permute-start.11
  884.0 9.2 collective-permute-start.12
  890.0 3.2 collective-permute-start.13
  893.3 6.2 collective-permute-start.14
  894.6 5.5 collective-permute-start.15
  938.5 63.0 %copy-start.14 = (pred[3,3,128]{2,1,0:T(4,128)(4,1)S(1)}, pred[3,3,128]{2,1,0:T(4,128)(4,1)}, u32[]{:S(2)}) copy-start(pred[3,3,128]{2,1,0:T(4,128)(4,1)} %iota_compare_fusion.8) | copy-start | bytes 3460
  938.6 8.9 collective-permute-start.16
  944.6 3.1 collective-permute-start.17
  947.8 5.8 collective-permute-start.18
  949.1 5.5 collective-permute-start.19
  993.3 29.1 %copy-start.7 = (f32[3,8,8,512]{3,2,1,0:T(8,128)}, f32[3,8,8,512]{3,2,1,0:T(8,128)S(1)}, u32[]{:S(2)}) copy-start(f32[3,8,8,512]{3,2,1,0:T(8,128)S(1)} %multiply_add_fusion) | copy-start | bytes 1179652
  1001.5 7.4 collective-permute-start.20
  1007.0 4.9 collective-permute-start.21
  1011.9 5.0 collective-permute-start.22
  1015.6 4.4 collective-permute-start.23
where the time goes:
time: 1020 us
  local copies, waits for them, and re-layouts  689 us (68%)
  blocking collectives  133 us (13%)
  other arithmetic  85.8 us (8%)
  starting transfers between devices  75 us (7%)
  waiting for transfers between devices  24.1 us (2%)
  between operations  15.1 us (1%)
    gather x8, local copies, waits for them, and re-layouts, fetch_entries(): picked = table_rows[positions // lane_count]  683 us
    psum x16, blocking collectives, one_axis_at_a_time(): return functools.reduce(lax.psum, axes, shard)  133 us
    reduce_sum x4, other arithmetic, fetch_entries(): return jnp.sum(jnp.where(chosen, picked, jnp.zeros_like(picked)), axis=-1)  70.3 us
    ppermute x12, starting transfers between devices, with_halo(): before = lax.ppermute(last, axis, up)  43.2 us
    ppermute x12, starting transfers between devices, with_halo(): after = lax.ppermute(leading, axis, down)  31.8 us
  transfers between devices with their start and end apart: 24, of which 14 were waited for; matrix products, arithmetic and copies ran while one was open for 0% of the time, Pallas kernels for 0%

commit v1 on v0

v1 whole, which is shorter than its diff:
```python
import functools

import jax
import jax.numpy as jnp
from jax import lax
from jax.experimental import pallas as pl
from jax.experimental.pallas import tpu as pltpu
from jax.sharding import PartitionSpec as P

DOM = "dom"
SLAB = "slab"
BOTH = ("dom", "slab")
ITERS = 4
COEF = 0.5
CENTRE = 7.125
SPREAD = 6.875
VMEM = 56 * 2**20


def with_halo(shard, sides, width):
    for axis, dim in sides:
        peers, length = (lax.axis_size(axis), shard.shape[dim])
        up = [(i, i + 1) for i in range(peers - 1)]
        down = [(j, i) for i, j in up]
        last = lax.slice_in_dim(shard, length - width, length, axis=dim)
        leading = lax.slice_in_dim(shard, 0, width, axis=dim)
        before = lax.ppermute(last, axis, up)
        after = lax.ppermute(leading, axis, down)
        shard = jnp.concatenate([before, shard, after], axis=dim)
    return shard


def two_pieces(table):
    high = table.astype(jnp.bfloat16)
    low = (table - high.astype(jnp.float32)).astype(jnp.bfloat16)
    return high, low


def look_up(pieces_ref, groups, across, group):
    width = across.shape[1]
    hot = lax.broadcasted_iota(jnp.int32, (256, width), 0) == across
    hot = jnp.where(hot, 1.0, 0.0).astype(jnp.bfloat16)
    picked = jnp.dot(pieces_ref[...], hot, preferred_element_type=jnp.float32)
    picked = picked[:groups] + picked[groups:]
    apart = group - lax.broadcasted_iota(jnp.int32, (8, width), 0)
    total = jnp.zeros((8, width), jnp.float32)
    for k in range(groups // 8):
        total = jnp.where(apart == 8 * k, picked[8 * k : 8 * k + 8], total)
    return total


def pair_of_rows(ref, row):
    return jnp.concatenate([ref[pl.ds(row, 1), :], ref[pl.ds(row + 1, 1), :]], axis=1)


def slots_kernel(heat_ref, position_ref, out_ref, pieces_ref):
    table = jnp.concatenate([heat_ref[:64], heat_ref[64:]], axis=1)
    pieces_ref[:64], pieces_ref[64:] = two_pieces(table)

    def step(i, carry):
        for pair in range(8):
            row = 16 * i + 2 * pair
            k = pair_of_rows(position_ref, row)
            across = (k >> 13) * 128 + (k & 127)
            found = look_up(pieces_ref, 64, across, (k >> 7) & 63)
            found = jnp.sum(found, axis=0, keepdims=True)
            out_ref[pl.ds(row, 1), :] = found[:, :128]
            out_ref[pl.ds(row + 1, 1), :] = found[:, 128:]
        return carry

    lax.fori_loop(0, position_ref.shape[0] // 16, step, 0)


def interp_kernel(slots_ref, shift_ref, bucket_ref, factor_ref, out_ref, pieces_ref):
    for h in range(9):
        table = jnp.concatenate(
            [slots_ref[64 * h : 64 * h + 32], slots_ref[64 * h + 32 : 64 * h + 64]], axis=1
        )
        pieces_ref[32 * h : 32 * h + 32], pieces_ref[288 + 32 * h : 320 + 32 * h] = two_pieces(table)

    def step(i, carry):
        for pair in range(4):
            row = 8 * i + 2 * pair
            total = jnp.zeros((8, 256), jnp.float32)
            for corner in range(4):
                k = pair_of_rows(bucket_ref.at[corner], row)
                holder = pair_of_rows(shift_ref.at[corner], row)
                across = ((k >> 12) & 1) * 128 + (k & 127)
                found = look_up(pieces_ref, 288, across, holder * 32 + ((k >> 7) & 31))
                total = total + found * pair_of_rows(factor_ref.at[corner], row)
            total = jnp.sum(total, axis=0, keepdims=True)
            out_ref[pl.ds(row, 1), :] = total[:, :128]
            out_ref[pl.ds(row + 1, 1), :] = total[:, 128:]
        return carry

    lax.fori_loop(0, out_ref.shape[0] // 8, step, 0)


def call(kernel, rows, scratch, *args):
    return pl.pallas_call(
        kernel,
        out_shape=jax.ShapeDtypeStruct((rows, 128), jnp.float32),
        scratch_shapes=scratch,
        compiler_params=pltpu.CompilerParams(vmem_limit_bytes=VMEM),
    )(*args)


def fetch_entries(source_table, positions):
    entry_count = source_table.shape[0]
    table_rows = source_table.reshape(entry_count // 128, 128)
    picked = table_rows[positions // 128]
    chosen = jnp.arange(128, dtype=jnp.int32) == (positions % 128)[..., None]
    return jnp.sum(jnp.where(chosen, picked, jnp.zeros_like(picked)), axis=-1)


def spread_entries(values, positions, entry_count):
    row_count = entry_count // 128
    row_hot = ((positions // 128)[:, None] == jnp.arange(row_count)[None, :]).astype(jnp.float32)
    lane_hot = ((positions % 128)[:, None] == jnp.arange(128)[None, :]).astype(jnp.float32)
    weighted = values[:, :, None] * lane_hot[None]
    summed = jnp.einsum("kh,ckl->chl", row_hot, weighted, precision=lax.Precision.HIGHEST)
    return summed.reshape(values.shape[0], entry_count)


def scaled_operate(field, rigidity):
    inner = field[:, 1:-1, 1:-1, :]
    along_z = jnp.pad(inner, ((0, 0), (0, 0), (0, 0), (1, 1)))
    beside = field[:, 2:, 1:-1, :] + field[:, :-2, 1:-1, :]
    beside = beside + field[:, 1:-1, 2:, :] + field[:, 1:-1, :-2, :]
    beside = beside + along_z[:, :, :, 2:] + along_z[:, :, :, :-2]
    return ((6.0 - CENTRE + rigidity)[None] * inner - beside) * (1.0 / SPREAD)


def coefficients(moments):
    m = list(moments[:7])
    m[2], m[3] = 2.0 * m[2] - m[0], 2.0 * m[3] - m[1]
    m[4], m[5], m[6] = 2.0 * m[4] - m[0], 2.0 * m[5] - m[1], 2.0 * m[6] - m[0]
    gram = [[0.5 * (m[i + j] + m[abs(i - j)]) for j in range(4)] for i in range(4)]
    h = [[None] * 4 for _ in range(4)]
    for i in range(4):
        h[i][0] = gram[i][1]
        h[i][1] = 0.5 * (gram[i][0] + gram[i][2])
        h[i][2] = 0.5 * (gram[i][1] + gram[i][3])
    for i in range(3):
        h[i][3] = h[3][i]
    h[3][3] = moments[7]
    image = [[CENTRE * gram[i][j] + SPREAD * h[i][j] for j in range(4)] for i in range(4)]

    def form(matrix, v):
        n = len(v)
        return sum(
            (matrix[i][j] if i == j else 2.0 * matrix[i][j]) * v[i] * v[j]
            for i in range(n)
            for j in range(i, n)
        )

    one = jnp.ones_like(m[0])
    zero = jnp.zeros_like(m[0])
    x, r, p = [], [one], [one]
    rr = form(gram, r)
    for step in range(ITERS):
        alpha = rr / form(image, p)
        x = [(x[i] if i < len(x) else zero) + alpha * p[i] for i in range(len(p))]
        if step + 1 == ITERS:
            break
        shifted = [zero] * (len(p) + 1)
        for i, v in enumerate(p):
            shifted[i] = shifted[i] + CENTRE * v
            if i == 0:
                shifted[1] = shifted[1] + SPREAD * v
            else:
                shifted[i - 1] = shifted[i - 1] + 0.5 * SPREAD * v
                shifted[i + 1] = shifted[i + 1] + 0.5 * SPREAD * v
        r = [(r[i] if i < len(r) else zero) - alpha * shifted[i] for i in range(len(shifted))]
        new = form(gram, r)
        beta = new / rr
        p = [r[i] + beta * (p[i] if i < len(p) else zero) for i in range(len(r))]
        rr = new
    return x


def on_device(heat, emitting, shift, bucket, factors, rigidity, wet_position, wet_tally, accepting):
    dom_pos, slab_pos = lax.axis_index(DOM), lax.axis_index(SLAB)
    doms, slabs = lax.axis_size(DOM), lax.axis_size(SLAB)
    slots = call(
        slots_kernel,
        576,
        [pltpu.VMEM((128, 256), jnp.bfloat16)],
        heat.reshape(128, 128),
        emitting.reshape(576, 128),
    ).reshape(3, 3, 8192)
    wide = with_halo(rigidity, ((DOM, 0), (SLAB, 1)), 3)
    gathered = with_halo(slots, ((DOM, 0), (SLAB, 1)), 1)
    received = gathered[::2, ::2, :].reshape(576, 128)
    interp = call(
        interp_kernel,
        256,
        [pltpu.VMEM((576, 256), jnp.bfloat16)],
        received,
        shift.reshape(4, 256, 128),
        bucket.reshape(4, 256, 128),
        factors.reshape(4, 256, 128),
    ).reshape(8, 8, 512)
    deep = with_halo(interp, ((DOM, 0), (SLAB, 1)), 5)
    along_z = jnp.pad(deep[1:-1, 1:-1], ((0, 0), (0, 0), (1, 1)))
    load = COEF * jnp.stack(
        [
            deep[2:, 1:-1] - deep[:-2, 1:-1],
            deep[1:-1, 2:] - deep[1:-1, :-2],
            along_z[:, :, 2:] - along_z[:, :, :-2],
        ]
    )
    x_at = dom_pos * 8 - 4 + jnp.arange(16, dtype=jnp.int32)
    y_at = slab_pos * 8 - 4 + jnp.arange(16, dtype=jnp.int32)
    inside = ((x_at >= 0) & (x_at < 8 * doms))[:, None] & ((y_at >= 0) & (y_at < 8 * slabs))[None]

    def keep(field, depth):
        cut = inside[4 - depth : 12 + depth, 4 - depth : 12 + depth]
        return jnp.where(cut[None, :, :, None], field, jnp.zeros_like(field))

    def near(depth):
        return wide[3 - depth : 11 + depth, 3 - depth : 11 + depth]

    w0 = keep(load, 4)
    w1 = keep(scaled_operate(w0, near(3)), 3)
    w2 = keep(2.0 * scaled_operate(w1, near(2)) - w0[:, 2:-2, 2:-2], 2)
    w3 = keep(2.0 * scaled_operate(w2, near(1)) - w1[:, 2:-2, 2:-2], 1)
    last = scaled_operate(w3, near(0))
    w0, w1, w2, w3 = w0[:, 4:-4, 4:-4], w1[:, 3:-3, 3:-3], w2[:, 2:-2, 2:-2], w3[:, 1:-1, 1:-1]
    pairs = ((w0, w0), (w0, w1), (w1, w1), (w1, w2), (w2, w2), (w2, w3), (w3, w3), (w3, last))
    moments = lax.psum(jnp.stack([jnp.sum(a * b) for a, b in pairs]), BOTH)
    c = coefficients([moments[i] for i in range(8)])
    solution = c[0] * w0 + c[1] * w1 + c[2] * w2 + c[3] * w3

    flat = solution.reshape(3, -1)
    surface = jnp.stack([fetch_entries(flat[a], wet_position[0]) for a in range(3)])
    live = jnp.arange(128, dtype=jnp.int32)[None, None, :] < wet_tally[0].reshape(3, 3)[:, :, None]
    surface = jnp.where(live[None], surface, jnp.zeros_like(surface))
    returned = with_halo(surface, ((DOM, 1), (SLAB, 2)), 1)
    arrived = returned[:, ::2, ::2, :]
    thermal_disp = spread_entries(arrived.reshape(3, -1), accepting[0].reshape(-1), heat.shape[0])
    return solution, thermal_disp


def solution(mesh):
    in_specs = (
        P(BOTH),
        P(BOTH, None, None, None),
        P(None, DOM, SLAB, None),
        P(None, DOM, SLAB, None),
        P(None, DOM, SLAB, None),
        P(DOM, SLAB, None),
        P(BOTH, None, None, None),
        P(BOTH, None),
        P(BOTH, None, None, None),
    )
    out_specs = (P(None, DOM, SLAB, None), P(None, BOTH))
    return jax.shard_map(on_device, mesh=mesh, in_specs=in_specs, out_specs=out_specs, check_vma=False)
```

time: 1020 us -> 258 us (0.25)
  local copies, waits for them, and re-layouts: 689 us -> 32.3 us
  other arithmetic: 85.8 us -> 13.6 us
  Pallas kernels: 0 us -> 60.8 us
  blocking collectives: 133 us -> 72.5 us
  starting transfers between devices: 75 us -> 43.4 us
    gather x8 -> x3, local copies, waits for them, and re-layouts: 683 us -> 7.33 us  [fetch_entries(): picked = table_rows[positions // 128]]
    reduce_sum x4 -> x1, other arithmetic: 70.3 us -> 0.75 us  [fetch_entries(): return jnp.sum(jnp.where(chosen, picked, jnp.zeros_like(picked)), axis=-1)]
    pallas_call x0 -> x2, Pallas kernels: none -> 60.8 us  [call(): pl.pallas_call(kernel, out_shape=jax.ShapeDtypeStruct((rows, 128), jnp.fl...]
    psum x16 -> x1, blocking collectives: 133 us -> 72.5 us  [on_device(): moments = lax.psum(jnp.stack([jnp.sum(a * b) for a, b in pairs]), BOTH)]
    ppermute x12 -> x8, starting transfers between devices: 31.8 us -> 12.8 us  [with_halo(): after = lax.ppermute(leading, axis, down)]
    ppermute x12 -> x8, starting transfers between devices: 43.2 us -> 30.6 us  [with_halo(): before = lax.ppermute(last, axis, up)]
  transfers between devices with their start and end apart: 24 -> 16, of which waited for: 14 -> 6; matrix products, arithmetic and copies ran while one was open for 0% -> 5% of each run, Pallas kernels for 0% -> 0%
where the time goes in v1:
time: 258 us; the launch traced here: 255 us
  blocking collectives  72.5 us (28%)
  Pallas kernels  60.8 us (24%)
  starting transfers between devices  43.4 us (17%)
  local copies, waits for them, and re-layouts  32.3 us (13%)
  waiting for transfers between devices  17.5 us (7%)
  between operations  14.1 us (5%)
  other arithmetic  13.6 us (5%)
    psum x1, blocking collectives, on_device(): moments = lax.psum(jnp.stack([jnp.sum(a * b) for a, b in pairs]), BOTH)  72.5 us
    pallas_call x2, Pallas kernels, call(): pl.pallas_call(kernel, out_shape=jax.ShapeDtypeStruct((rows, 128), jnp.fl...  60.8 us
    ppermute x8, starting transfers between devices, with_halo(): before = lax.ppermute(last, axis, up)  30.6 us
    ppermute x8, waiting for transfers between devices, with_halo(): after = lax.ppermute(leading, axis, down)  14.1 us
    ppermute x8, starting transfers between devices, with_halo(): after = lax.ppermute(leading, axis, down)  12.8 us
    gather x3, local copies, waits for them, and re-layouts, fetch_entries(): picked = table_rows[positions // 128]  7.33 us
  transfers between devices with their start and end apart: 16, of which 6 were waited for; matrix products, arithmetic and copies ran while one was open for 5% of the time, Pallas kernels for 0%

profile of v1, /device:TPU:1, one launch (start us, length us, event | category | flops | bytes accessed | tf_op | source)
XLA Modules:
  0.0 255.2 jit_solution(5707640480974972337)
XLA Ops:
  0.7 13.5 %shard_map.104 = f32[576,128]{1,0:T(8,128)} custom-call(f32[128,128]{1,0:T(8,128)} %bitcast.71, s32[576,128]{1,0:T(8,128)} %bitcast.69), custom_call_target="tpu_custom_call" | custom-call | tf_op jit(solution)/shard_map/pallas_call | solution.py:100
  14.1 1.0 fusion.46
  15.1 4.6 %collective-permute-start = (f32[1,3,8192]{2,1,0:T(4,128)S(1)}, f32[1,3,8192]{2,1,0:T(4,128)S(1)}, u32[]{:S(2)}, u32[]{:S(2)}) collective-permute-start(f32[1,3,8192]{2,1,0:T(4,128)S(1)} %slice.239), channel_id=1, source_target_pairs={{0,16},{16,32},{32,48},{48,64},{64,80},{80,96},{96,112},{1,17},{17... | collective-permute-start | bytes 294920 | tf_op jit(solution)/shard_map/ppermute | solution.py:27
  19.8 1.9 collective-permute-start.1
  21.7 3.6 %collective-permute-start.8 = (f32[3,8,512]{2,1,0:T(8,128)S(1)}, f32[3,8,512]{2,1,0:T(8,128)S(1)}, u32[]{:S(2)}, u32[]{:S(2)}) collective-permute-start(f32[3,8,512]{2,1,0:T(8,128)S(1)} %get-tuple-element.38), channel_id=1, source_target_pairs={{0,16},{16,32},{32,48},{48,64},{64,80},{80,96},{96,112},{1,17},{17... | collective-permute-start | bytes 147464 | tf_op jit(solution)/shard_map/ppermute | solution.py:27
  25.4 1.9 collective-permute-start.9
  29.4 1.1 reshape.303
  31.5 3.7 %collective-permute-start.10 = (f32[14,3,512]{2,1,0:T(4,128)}, f32[14,3,512]{2,1,0:T(4,128)}, u32[]{:S(2)}, u32[]{:S(2)}) collective-permute-start(f32[14,3,512]{2,1,0:T(4,128)} %get-tuple-element.33), channel_id=1, source_target_pairs={{0,1},{1,2},{2,3},{3,4},{4,5},{5,6},{6,7},{7,8},{8,9},{9,10},{10,1... | collective-permute-start | bytes 258056 | tf_op jit(solution)/shard_map/ppermute | solution.py:27
  35.2 1.3 collective-permute-start.11
  36.7 1.0 fusion.43
  37.7 4.6 %collective-permute-start.2 = (f32[5,1,8192]{2,1,0:T(1,128)}, f32[5,1,8192]{2,1,0:T(1,128)}, u32[]{:S(2)}, u32[]{:S(2)}) collective-permute-start(f32[5,1,8192]{2,1,0:T(1,128)} %get-tuple-element.22), channel_id=1, source_target_pairs={{0,1},{1,2},{2,3},{3,4},{4,5},{5,6},{6,7},{7,8},{8,9},{9,10},{10,1... | collective-permute-start | bytes 491528 | tf_op jit(solution)/shard_map/ppermute | solution.py:27
  42.4 1.3 collective-permute-start.3
  45.7 0.8 reshape.305.shift_ref
  46.5 0.8 reshape.306.bucket_ref
  47.3 0.8 reshape.307.factor_ref
  48.8 1.1 pad_maximum_fusion.2
  49.9 1.4 pad_maximum_fusion
  51.3 3.4 %slice.244 = f32[3,3,8192]{2,1,0:T(4,128)S(1)} slice(f32[5,5,8192]{2,1,0:T(8,128)S(1)} %pad_maximum_fusion), slice={[0:5:2], [0:5:2], [0:8192:1]} | slice | bytes 589824 | tf_op jit(solution)/shard_map/slice | solution.py:194
  54.7 0.9 reshape.304.slots_ref
  55.7 47.3 %shard_map.105 = f32[256,128]{1,0:T(8,128)} custom-call(f32[576,128]{1,0:T(8,128)} %reshape.304.slots_ref, s32[4,256,128]{2,1,0:T(8,128)} %reshape.305.shift_ref, s32[4,256,128]{2,1,0:T(8,128)} %reshape.306.bucket_ref, f32[4,256,128]{2,1,0:T(8,128)} %reshape.307.factor_ref), custom_call_target="tpu_custom_call" | custom-call | tf_op jit(solution)/shard_map/pallas_call | solution.py:100
  103.0 1.0 fusion.49
  104.0 4.4 %collective-permute-start.4 = (f32[5,8,512]{2,1,0:T(8,128)S(1)}, f32[5,8,512]{2,1,0:T(8,128)S(1)}, u32[]{:S(2)}, u32[]{:S(2)}) collective-permute-start(f32[5,8,512]{2,1,0:T(8,128)S(1)} %slice.246), channel_id=1, source_target_pairs={{0,16},{16,32},{32,48},{48,64},{64,80},{80,96},{96,112},{1,17},{17... | collective-permute-start | bytes 245768 | tf_op jit(solution)/shard_map/ppermute | solution.py:27
  109.2 0.9 reshape.308
  110.1 1.9 collective-permute-start.5
  112.1 3.8 %collective-permute-done.5 = f32[5,8,512]{2,1,0:T(8,128)S(1)} collective-permute-done((f32[5,8,512]{2,1,0:T(8,128)S(1)}, f32[5,8,512]{2,1,0:T(8,128)S(1)}, u32[]{:S(2)}, u32[]{:S(2)}) %collective-permute-start.5) | collective-permute-done | bytes 81952 | tf_op jit(solution)/shard_map/ppermute | solution.py:28
  116.0 4.2 %collective-permute-start.6 = (f32[18,5,512]{2,1,0:T(8,128)S(1)}, f32[18,5,512]{2,1,0:T(8,128)S(1)}, u32[]{:S(2)}, u32[]{:S(2)}) collective-permute-start(f32[18,5,512]{2,1,0:T(8,128)S(1)} %get-tuple-element.29), channel_id=1, source_target_pairs={{0,1},{1,2},{2,3},{3,4},{4,5},{5,6},{6,7},{7,8},{8,9},{9,10},{10,1... | collective-permute-start | bytes 552968 | tf_op jit(solution)/shard_map/ppermute | solution.py:27
  120.2 1.3 collective-permute-start.7
  121.5 3.3 %collective-permute-done.6 = f32[18,5,512]{2,1,0:T(8,128)S(1)} collective-permute-done((f32[18,5,512]{2,1,0:T(8,128)S(1)}, f32[18,5,512]{2,1,0:T(8,128)S(1)}, u32[]{:S(2)}, u32[]{:S(2)}) %collective-permute-start.6) | collective-permute-done | bytes 184352 | tf_op jit(solution)/shard_map/ppermute | solution.py:27
  124.9 4.1 %collective-permute-done.7 = f32[18,5,512]{2,1,0:T(8,128)S(1)} collective-permute-done((f32[18,5,512]{2,1,0:T(8,128)S(1)}, f32[18,5,512]{2,1,0:T(8,128)S(1)}, u32[]{:S(2)}, u32[]{:S(2)}) %collective-permute-start.7) | collective-permute-done | bytes 184352 | tf_op jit(solution)/shard_map/ppermute | solution.py:28
  130.6 1.0 fusion.7
  131.8 0.8 copy-done.2
  132.6 1.1 fusion.13
  134.4 1.0 fusion.22
  135.5 1.5 multiply_reduce_fusion.1
  137.0 5.1 %stack.63 = f32[8]{0:T(128)S(1)} concatenate(f32[1]{0:T(128)} %bitcast.5, f32[1]{0:T(128)} %bitcast.6, f32[1]{0:T(128)} %bitcast.7, f32[1]{0:T(128)} %bitcast.8, f32[1]{0:T(128)} %bitcast.9, f32[1]{0:T(128)} %bitcast.10, f32[1]{0:T(128)} %bitcast.11, f32[1]{0:T(128)} %bitcast.12), dimensions={0} | concatenate | bytes 64 | tf_op jit(solution)/shard_map/stack | solution.py:231
  142.1 72.5 %psum.7 = f32[8]{0:T(128)S(1)} all-reduce(f32[8]{0:T(128)S(1)} %stack.63), channel_id=1, replica_groups=mesh['dom'=8,'slab'=16] {'dom','slab'}, use_global_device_ids=true, to_apply=%region_8.9 | all-reduce | flops 8 | bytes 64 | tf_op jit(solution)/shard_map/psum | solution.py:231
  228.0 1.8 multiply_add_fusion
  229.9 2.4 gather_fusion
  232.3 2.4 gather_fusion.1
  234.8 2.4 gather_fusion.2
  238.0 3.0 %collective-permute-start.12 = (f32[3,1,3,128]{3,2,1,0:T(4,128)S(1)}, f32[3,1,3,128]{3,2,1,0:T(4,128)S(1)}, u32[]{:S(2)}, u32[]{:S(2)}) collective-permute-start(f32[3,1,3,128]{3,2,1,0:T(4,128)S(1)} %get-tuple-element.43), channel_id=1, source_target_pairs={{0,16},{16,32},{32,48},{48,64},{64,80},{80,96},{96,112},{1,17},{17... | collective-permute-start | bytes 13832 | tf_op jit(solution)/shard_map/ppermute | solution.py:27
  241.1 1.9 collective-permute-start.13
  243.0 3.0 %collective-permute-done.13 = f32[3,1,3,128]{3,2,1,0:T(4,128)S(1)} collective-permute-done((f32[3,1,3,128]{3,2,1,0:T(4,128)S(1)}, f32[3,1,3,128]{3,2,1,0:T(4,128)S(1)}, u32[]{:S(2)}, u32[]{:S(2)}) %collective-permute-start.13) | collective-permute-done | bytes 4640 | tf_op jit(solution)/shard_map/ppermute | solution.py:28
  246.0 2.4 collective-permute-start.14
  248.4 1.3 collective-permute-start.15
  249.7 3.0 %collective-permute-done.15 = f32[3,5,1,128]{3,2,1,0:T(1,128)S(1)} collective-permute-done((f32[3,5,1,128]{3,2,1,0:T(1,128)S(1)}, f32[3,5,1,128]{3,2,1,0:T(1,128)S(1)}, u32[]{:S(2)}, u32[]{:S(2)}) %collective-permute-start.15) | collective-permute-done | bytes 7712 | tf_op jit(solution)/shard_map/ppermute | solution.py:28
  253.2 1.0 fusion.14
  254.3 0.8 copy.18
  (98 shorter events, 11.5 us)
Async XLA Ops:
  0.6 21.1 %copy-start.7 = (f32[8,8,512]{2,1,0:T(8,128)S(1)}, f32[8,8,512]{2,1,0:T(8,128)}, u32[]{:S(2)}) copy-start(f32[8,8,512]{2,1,0:T(8,128)} %param.14) | copy-start | bytes 393220
  0.6 26.7 %copy-start.9 = (s32[1,3,3,128]{3,0,2,1:T(1,128)S(1)}, s32[1,3,3,128]{3,0,2,1:T(1,128)}, u32[]{:S(2)}) copy-start(s32[1,3,3,128]{3,0,2,1:T(1,128)} %param.15) | copy-start | bytes 13828
  0.7 27.2 %copy-start.15 = (s32[1,9]{1,0:T(1,128)S(1)}, s32[1,9]{1,0:T(1,128)}, u32[]{:S(2)}) copy-start(s32[1,9]{1,0:T(1,128)} %param.16) | copy-start | bytes 112
  15.1 21.4 %collective-permute-start = (f32[1,3,8192]{2,1,0:T(4,128)S(1)}, f32[1,3,8192]{2,1,0:T(4,128)S(1)}, u32[]{:S(2)}, u32[]{:S(2)}) collective-permute-start(f32[1,3,8192]{2,1,0:T(4,128)S(1)} %slice.239), channel_id=1, source_target_pairs={{0,16},{16,32},{32,48},{48,64},{64,80},{80,96},{96,112},{1,17},{17... | collective-permute-start | bytes 294920 | tf_op jit(solution)/shard_map/ppermute | solution.py:27
  19.8 16.9 %collective-permute-start.1 = (f32[1,3,8192]{2,1,0:T(4,128)S(1)}, f32[1,3,8192]{2,1,0:T(4,128)S(1)}, u32[]{:S(2)}, u32[]{:S(2)}) collective-permute-start(f32[1,3,8192]{2,1,0:T(4,128)S(1)} %slice.241), channel_id=1, source_target_pairs={{16,0},{32,16},{48,32},{64,48},{80,64},{96,80},{112,96},{17,1},{33... | collective-permute-start | bytes 294920 | tf_op jit(solution)/shard_map/ppermute | solution.py:28
  21.7 8.8 %collective-permute-start.8 = (f32[3,8,512]{2,1,0:T(8,128)S(1)}, f32[3,8,512]{2,1,0:T(8,128)S(1)}, u32[]{:S(2)}, u32[]{:S(2)}) collective-permute-start(f32[3,8,512]{2,1,0:T(8,128)S(1)} %get-tuple-element.38), channel_id=1, source_target_pairs={{0,16},{16,32},{32,48},{48,64},{64,80},{80,96},{96,112},{1,17},{17... | collective-permute-start | bytes 147464 | tf_op jit(solution)/shard_map/ppermute | solution.py:27
  25.4 5.4 %collective-permute-start.9 = (f32[3,8,512]{2,1,0:T(8,128)S(1)}, f32[3,8,512]{2,1,0:T(8,128)S(1)}, u32[]{:S(2)}, u32[]{:S(2)}) collective-permute-start(f32[3,8,512]{2,1,0:T(8,128)S(1)} %get-tuple-element.37), channel_id=1, source_target_pairs={{16,0},{32,16},{48,32},{64,48},{80,64},{96,80},{112,96},{17,1},{33... | collective-permute-start | bytes 147464 | tf_op jit(solution)/shard_map/ppermute | solution.py:28
  30.6 15.1 %copy-start.4 = (s32[4,8,8,512]{3,2,1,0:T(8,128)S(1)}, s32[4,8,8,512]{3,2,1,0:T(8,128)}, u32[]{:S(2)}) copy-start(s32[4,8,8,512]{3,2,1,0:T(8,128)} %param.11) | copy-start | bytes 1572868
  31.5 17.3 %collective-permute-start.10 = (f32[14,3,512]{2,1,0:T(4,128)}, f32[14,3,512]{2,1,0:T(4,128)}, u32[]{:S(2)}, u32[]{:S(2)}) collective-permute-start(f32[14,3,512]{2,1,0:T(4,128)} %get-tuple-element.33), channel_id=1, source_target_pairs={{0,1},{1,2},{2,3},{3,4},{4,5},{5,6},{6,7},{7,8},{8,9},{9,10},{10,1... | collective-permute-start | bytes 258056 | tf_op jit(solution)/shard_map/ppermute | solution.py:27
  35.2 13.6 %collective-permute-start.11 = (f32[14,3,512]{2,1,0:T(4,128)S(1)}, f32[14,3,512]{2,1,0:T(4,128)}, u32[]{:S(2)}, u32[]{:S(2)}) collective-permute-start(f32[14,3,512]{2,1,0:T(4,128)S(1)} %get-tuple-element.34), channel_id=1, source_target_pairs={{1,0},{2,1},{3,2},{4,3},{5,4},{6,5},{7,6},{8,7},{9,8},{10,9},{11,1... | collective-permute-start | bytes 258056 | tf_op jit(solution)/shard_map/ppermute | solution.py:28
  36.6 9.9 %copy-start.5 = (s32[4,8,8,512]{3,2,1,0:T(8,128)S(1)}, s32[4,8,8,512]{3,2,1,0:T(8,128)}, u32[]{:S(2)}) copy-start(s32[4,8,8,512]{3,2,1,0:T(8,128)} %param.12) | copy-start | bytes 1572868
  36.7 10.6 %copy-start.6 = (f32[4,8,8,512]{3,2,1,0:T(8,128)S(1)}, f32[4,8,8,512]{3,2,1,0:T(8,128)}, u32[]{:S(2)}) copy-start(f32[4,8,8,512]{3,2,1,0:T(8,128)} %param.13) | copy-start | bytes 1572868
  37.7 12.2 %collective-permute-start.2 = (f32[5,1,8192]{2,1,0:T(1,128)}, f32[5,1,8192]{2,1,0:T(1,128)}, u32[]{:S(2)}, u32[]{:S(2)}) collective-permute-start(f32[5,1,8192]{2,1,0:T(1,128)} %get-tuple-element.22), channel_id=1, source_target_pairs={{0,1},{1,2},{2,3},{3,4},{4,5},{5,6},{6,7},{7,8},{8,9},{9,10},{10,1... | collective-permute-start | bytes 491528 | tf_op jit(solution)/shard_map/ppermute | solution.py:27
  42.4 7.5 %collective-permute-start.3 = (f32[5,1,8192]{2,1,0:T(1,128)}, f32[5,1,8192]{2,1,0:T(1,128)}, u32[]{:S(2)}, u32[]{:S(2)}) collective-permute-start(f32[5,1,8192]{2,1,0:T(1,128)} %get-tuple-element.23), channel_id=1, source_target_pairs={{1,0},{2,1},{3,2},{4,3},{5,4},{6,5},{7,6},{8,7},{9,8},{10,9},{11,1... | collective-permute-start | bytes 491528 | tf_op jit(solution)/shard_map/ppermute | solution.py:28
  45.7 2.5 copy-start.14
  104.0 8.1 %collective-permute-start.4 = (f32[5,8,512]{2,1,0:T(8,128)S(1)}, f32[5,8,512]{2,1,0:T(8,128)S(1)}, u32[]{:S(2)}, u32[]{:S(2)}) collective-permute-start(f32[5,8,512]{2,1,0:T(8,128)S(1)} %slice.246), channel_id=1, source_target_pairs={{0,16},{16,32},{32,48},{48,64},{64,80},{80,96},{96,112},{1,17},{17... | collective-permute-start | bytes 245768 | tf_op jit(solution)/shard_map/ppermute | solution.py:27
  110.1 5.8 %collective-permute-start.5 = (f32[5,8,512]{2,1,0:T(8,128)S(1)}, f32[5,8,512]{2,1,0:T(8,128)S(1)}, u32[]{:S(2)}, u32[]{:S(2)}) collective-permute-start(f32[5,8,512]{2,1,0:T(8,128)S(1)} %slice.248), channel_id=1, source_target_pairs={{16,0},{32,16},{48,32},{64,48},{80,64},{96,80},{112,96},{17,1},{33... | collective-permute-start | bytes 245768 | tf_op jit(solution)/shard_map/ppermute | solution.py:28
  116.0 8.9 %collective-permute-start.6 = (f32[18,5,512]{2,1,0:T(8,128)S(1)}, f32[18,5,512]{2,1,0:T(8,128)S(1)}, u32[]{:S(2)}, u32[]{:S(2)}) collective-permute-start(f32[18,5,512]{2,1,0:T(8,128)S(1)} %get-tuple-element.29), channel_id=1, source_target_pairs={{0,1},{1,2},{2,3},{3,4},{4,5},{5,6},{6,7},{7,8},{8,9},{9,10},{10,1... | collective-permute-start | bytes 552968 | tf_op jit(solution)/shard_map/ppermute | solution.py:27
  120.2 8.8 %collective-permute-start.7 = (f32[18,5,512]{2,1,0:T(8,128)S(1)}, f32[18,5,512]{2,1,0:T(8,128)S(1)}, u32[]{:S(2)}, u32[]{:S(2)}) collective-permute-start(f32[18,5,512]{2,1,0:T(8,128)S(1)} %get-tuple-element.30), channel_id=1, source_target_pairs={{1,0},{2,1},{3,2},{4,3},{5,4},{6,5},{7,6},{8,7},{9,8},{10,9},{11,1... | collective-permute-start | bytes 552968 | tf_op jit(solution)/shard_map/ppermute | solution.py:28
  129.9 0.7 copy-start.11
  131.6 1.0 copy-start.2
  131.6 1.0 copy-start.10
  133.7 1.8 copy-start
  133.7 0.7 copy-start.12
  135.4 1.6 copy-start.1
  135.5 6.6 %copy-start.8 = (s32[3,3,128]{2,1,0:T(4,128)S(1)}, s32[3,3,128]{2,1,0:T(4,128)}, u32[]{:S(2)}) copy-start(s32[3,3,128]{2,1,0:T(4,128)} %reduce.2) | copy-start | bytes 13828
  229.8 2.5 copy-start.3
  237.2 0.8 copy-start.13
  238.0 5.0 %collective-permute-start.12 = (f32[3,1,3,128]{3,2,1,0:T(4,128)S(1)}, f32[3,1,3,128]{3,2,1,0:T(4,128)S(1)}, u32[]{:S(2)}, u32[]{:S(2)}) collective-permute-start(f32[3,1,3,128]{3,2,1,0:T(4,128)S(1)} %get-tuple-element.43), channel_id=1, source_target_pairs={{0,16},{16,32},{32,48},{48,64},{64,80},{80,96},{96,112},{1,17},{17... | collective-permute-start | bytes 13832 | tf_op jit(solution)/shard_map/ppermute | solution.py:27
  241.1 4.9 %collective-permute-start.13 = (f32[3,1,3,128]{3,2,1,0:T(4,128)S(1)}, f32[3,1,3,128]{3,2,1,0:T(4,128)S(1)}, u32[]{:S(2)}, u32[]{:S(2)}) collective-permute-start(f32[3,1,3,128]{3,2,1,0:T(4,128)S(1)} %get-tuple-element.44), channel_id=1, source_target_pairs={{16,0},{32,16},{48,32},{64,48},{80,64},{96,80},{112,96},{17,1},{33... | collective-permute-start | bytes 13832 | tf_op jit(solution)/shard_map/ppermute | solution.py:28
  246.0 3.7 %collective-permute-start.14 = (f32[3,5,1,128]{3,2,1,0:T(1,128)S(1)}, f32[3,5,1,128]{3,2,1,0:T(1,128)S(1)}, u32[]{:S(2)}, u32[]{:S(2)}) collective-permute-start(f32[3,5,1,128]{3,2,1,0:T(1,128)S(1)} %get-tuple-element.41), channel_id=1, source_target_pairs={{0,1},{1,2},{2,3},{3,4},{4,5},{5,6},{6,7},{7,8},{8,9},{9,10},{10,1... | collective-permute-start | bytes 23048 | tf_op jit(solution)/shard_map/ppermute | solution.py:27
  248.4 4.4 %collective-permute-start.15 = (f32[3,5,1,128]{3,2,1,0:T(1,128)S(1)}, f32[3,5,1,128]{3,2,1,0:T(1,128)S(1)}, u32[]{:S(2)}, u32[]{:S(2)}) collective-permute-start(f32[3,5,1,128]{3,2,1,0:T(1,128)S(1)} %get-tuple-element.42), channel_id=1, source_target_pairs={{1,0},{2,1},{3,2},{4,3},{5,4},{6,5},{7,6},{8,7},{9,8},{10,9},{11,1... | collective-permute-start | bytes 23048 | tf_op jit(solution)/shard_map/ppermute | solution.py:28

commit v2 on v1

v2 whole, which is shorter than its diff:
```python
import functools

import jax
import jax.numpy as jnp
from jax import lax
from jax.experimental import pallas as pl
from jax.experimental.pallas import tpu as pltpu
from jax.sharding import PartitionSpec as P

DOM = "dom"
SLAB = "slab"
BOTH = ("dom", "slab")
MESH = pl.DeviceIdType.MESH
ITERS = 4
COEF = 0.5
CENTRE = 7.125
SPREAD = 6.875
F32 = jnp.float32
BF16 = jnp.bfloat16


def two_pieces(table):
    high = table.astype(BF16)
    low = (table - high.astype(F32)).astype(BF16)
    return high, low


def one_hot(across):
    width = across.shape[1]
    hot = lax.broadcasted_iota(jnp.int32, (256, width), 0) == across
    return jnp.where(hot, 1.0, 0.0).astype(BF16)


def pick_group(picked, groups, group):
    width = group.shape[1]
    picked = picked[:groups] + picked[groups:]
    apart = group - lax.broadcasted_iota(jnp.int32, (8, width), 0)
    total = jnp.zeros((8, width), F32)
    for k in range(groups // 8):
        total = jnp.where(apart == 8 * k, picked[8 * k : 8 * k + 8], total)
    return total


def look_up(pieces_ref, groups, across, group):
    picked = jnp.dot(pieces_ref[...], one_hot(across), preferred_element_type=F32)
    return pick_group(picked, groups, group)


def coefficients(moments):
    m = list(moments[:7])
    m[2], m[3] = 2.0 * m[2] - m[0], 2.0 * m[3] - m[1]
    m[4], m[5], m[6] = 2.0 * m[4] - m[0], 2.0 * m[5] - m[1], 2.0 * m[6] - m[0]
    gram = [[0.5 * (m[i + j] + m[abs(i - j)]) for j in range(4)] for i in range(4)]
    h = [[None] * 4 for _ in range(4)]
    for i in range(4):
        h[i][0] = gram[i][1]
        h[i][1] = 0.5 * (gram[i][0] + gram[i][2])
        h[i][2] = 0.5 * (gram[i][1] + gram[i][3])
    for i in range(3):
        h[i][3] = h[3][i]
    h[3][3] = moments[7]
    image = [[CENTRE * gram[i][j] + SPREAD * h[i][j] for j in range(4)] for i in range(4)]

    def form(matrix, v):
        n = len(v)
        return sum(
            (matrix[i][j] if i == j else 2.0 * matrix[i][j]) * v[i] * v[j]
            for i in range(n)
            for j in range(i, n)
        )

    one = jnp.ones_like(m[0])
    zero = jnp.zeros_like(m[0])
    x, r, p = [], [one], [one]
    rr = form(gram, r)
    for step in range(ITERS):
        alpha = rr / form(image, p)
        x = [(x[i] if i < len(x) else zero) + alpha * p[i] for i in range(len(p))]
        if step + 1 == ITERS:
            break
        shifted = [zero] * (len(p) + 1)
        for i, v in enumerate(p):
            shifted[i] = shifted[i] + CENTRE * v
            if i == 0:
                shifted[1] = shifted[1] + SPREAD * v
            else:
                shifted[i - 1] = shifted[i - 1] + 0.5 * SPREAD * v
                shifted[i + 1] = shifted[i + 1] + 0.5 * SPREAD * v
        r = [(r[i] if i < len(r) else zero) - alpha * shifted[i] for i in range(len(shifted))]
        new = form(gram, r)
        beta = new / rr
        p = [r[i] + beta * (p[i] if i < len(p) else zero) for i in range(len(r))]
        rr = new
    return x


def half_turn(tile):
    return pltpu.roll(tile, 4, 0)


def low_half(tile):
    return lax.broadcasted_iota(jnp.int32, tile.shape, 0) < 4


def pack_halos(block, side, corner, fifth):
    for x in range(4):
        near, far = block[x], block[x + 4]
        side[0, x] = jnp.where(low_half(near), near, half_turn(far))
        side[1, x] = jnp.where(low_half(near), half_turn(near), far)
    if fifth:
        for x in range(8):
            side[0, 4, x : x + 1] = block[x, 4:5]
            side[1, 4, x : x + 1] = block[x, 3:4]
    for a in range(2):
        for j in range(2):
            near, far = block[4 * a + j], block[4 * a + 2 + j]
            corner[a, 0, j] = jnp.where(low_half(near), near, half_turn(far))
            corner[a, 1, j] = jnp.where(low_half(near), half_turn(near), far)


def unpack_halos(block, side, dom, corner, wide):
    def put(at, middle, left, right):
        turned = half_turn(middle)
        wide[at, 0:8] = jnp.where(low_half(turned), left, turned)
        wide[at, 8:16] = jnp.where(low_half(turned), turned, right)

    for x in range(8):
        left, right = side[0, x % 4], side[1, x % 4]
        if x < 4:
            right = half_turn(right)
        else:
            left = half_turn(left)
        put(5 + x, block[x], left, right)
    for a in range(2):
        for t in range(5):
            u = t - 1 if a == 0 else t
            if 0 <= u < 4:
                left, right = corner[a, 0, u % 2], corner[a, 1, u % 2]
                if u < 2:
                    right = half_turn(right)
                else:
                    left = half_turn(left)
            else:
                left = right = jnp.zeros((8, 512), F32)
            put(t if a == 0 else 13 + t, dom[a, t], left, right)


def kernel(
    doms,
    slabs,
    heat,
    emitting,
    shift_hbm,
    bucket_hbm,
    factor_hbm,
    rigidity,
    wet_position,
    wet_tally,
    accepting,
    disp,
    spread,
    shift,
    bucket,
    factor,
    heat_pieces,
    slots_out,
    slots_in,
    pieces,
    interp,
    side_out,
    side_in,
    dom_in,
    corner_out,
    corner_in,
    rig_side_out,
    rig_side_in,
    rig_dom_in,
    rig_corner_out,
    rig_corner_in,
    wide,
    rig_wide,
    basis,
    centre,
    dom_moments,
    slab_moments,
    wet_pieces,
    wet_out,
    wet_in,
    load_sem,
    slot_send,
    slot_recv,
    halo_send,
    halo_recv,
    rig_send,
    rig_recv,
    wet_send,
    wet_recv,
    dom_send,
    dom_recv,
    slab_send,
    slab_recv,
):
    d, s = lax.axis_index(DOM), lax.axis_index(SLAB)

    def exists(a, b):
        return (d + a >= 1) & (d + a <= doms) & (s + b >= 1) & (s + b <= slabs)

    loads = [
        pltpu.make_async_copy(src, dst, load_sem.at[i])
        for i, (src, dst) in enumerate(((shift_hbm, shift), (bucket_hbm, bucket), (factor_hbm, factor)))
    ]
    for load in loads:
        load.start()

    barrier = pltpu.get_barrier_semaphore()
    for k in range(1, doms):
        pl.semaphore_signal(barrier, inc=1, device_id=(lax.rem(d + k, doms), s), device_id_type=MESH)
    for k in range(1, slabs):
        pl.semaphore_signal(barrier, inc=1, device_id=(d, lax.rem(s + k, slabs)), device_id_type=MESH)
    expected = doms + slabs - 2
    for a in (0, 2):
        for b in (0, 2):

            @pl.when(exists(a, b))
            def _():
                pl.semaphore_signal(
                    barrier, inc=1, device_id=(d + (a - 1), s + (b - 1)), device_id_type=MESH
                )

            expected = expected + exists(a, b).astype(jnp.int32)

    def halo_copies(block, s_out, s_in, d_in, c_out, c_in, send, recv):
        found = []
        for a in range(3):
            for b in range(3):
                if a == 1 and b == 1:
                    continue
                if a == 1:
                    src, dst = s_out.at[b // 2], s_in.at[1 - b // 2]
                elif b == 1:
                    src, dst = block.at[pl.ds(3 if a == 2 else 0, 5)], d_in.at[1 - a // 2]
                else:
                    src, dst = c_out.at[a // 2, b // 2], c_in.at[1 - a // 2, 1 - b // 2]
                j = 3 * a + b
                copy = pltpu.make_async_remote_copy(
                    src_ref=src,
                    dst_ref=dst,
                    send_sem=send.at[j],
                    recv_sem=recv.at[8 - j],
                    device_id=(d + (a - 1), s + (b - 1)),
                    device_id_type=MESH,
                )
                found.append((a, b, copy))
        return found

    def start_all(copies):
        for a, b, copy in copies:

            @pl.when(exists(a, b))
            def _():
                copy.start()

    def receive_all(copies):
        for a, b, copy in copies:

            @pl.when(exists(2 - a, 2 - b))
            def _():
                copy.wait_recv()

    def finish_all(copies):
        for a, b, copy in copies:

            @pl.when(exists(a, b))
            def _():
                copy.wait_send()

    def clear_missing(s_in, d_in, c_in):
        for a in range(3):
            for b in range(3):
                if a == 1 and b == 1:
                    continue

                @pl.when(jnp.logical_not(exists(a, b)))
                def _():
                    if a == 1:
                        s_in[b // 2] = jnp.zeros((5, 8, 512), F32)
                    elif b == 1:
                        d_in[a // 2] = jnp.zeros((5, 8, 512), F32)
                    else:
                        c_in[a // 2, b // 2] = jnp.zeros((2, 8, 512), F32)

    def clear_blocks(blocks):
        for j in range(9):
            if j == 4:
                continue

            @pl.when(jnp.logical_not(exists(j // 3, j % 3)))
            def _():
                blocks[j] = jnp.zeros(blocks.shape[1:], F32)

    heat_pieces[:64], heat_pieces[64:] = two_pieces(jnp.concatenate([heat[:64], heat[64:]], axis=1))
    pack_halos(rigidity, rig_side_out, rig_corner_out, False)
    for b in range(2):
        rig_side_out[b, 4] = jnp.zeros((8, 512), F32)
    clear_missing(rig_side_in, rig_dom_in, rig_corner_in)
    clear_missing(side_in, dom_in, corner_in)
    clear_blocks(slots_in)
    clear_blocks(wet_in)
    wet_out[...] = jnp.zeros(wet_out.shape, F32)
    pl.semaphore_wait(barrier, expected)
    rig_copies = halo_copies(
        rigidity, rig_side_out, rig_side_in, rig_dom_in, rig_corner_out, rig_corner_in, rig_send, rig_recv
    )
    start_all(rig_copies)

    def slot_copy(j):
        return pltpu.make_async_remote_copy(
            src_ref=slots_out.at[j],
            dst_ref=slots_in.at[8 - j],
            send_sem=slot_send.at[j],
            recv_sem=slot_recv.at[8 - j],
            device_id=(d + (j // 3 - 1), s + (j % 3 - 1)),
            device_id_type=MESH,
        )

    def slot_block(t, carry):
        j = lax.rem(t + 5, 9)
        a, b = j // 3, lax.rem(j, 3)

        def chunk(q, carry):
            for i in range(16):
                at = pl.multiple_of(4096 * q + 256 * i, 256)
                k = emitting[0, a, pl.ds(b, 1), pl.ds(at, 256)]
                across = (k >> 13) * 128 + (k & 127)
                found = look_up(heat_pieces, 64, across, (k >> 7) & 63)
                slots_out[j, pl.ds(16 * q + i, 1), :] = jnp.sum(found, axis=0, keepdims=True)
            return carry

        lax.fori_loop(0, 2, chunk, 0)

        @pl.when((j != 4) & exists(a, b))
        def _():
            slot_copy(j).start()

        return carry

    lax.fori_loop(0, 9, slot_block, 0)
    slots_in[4] = slots_out[4]
    for load in loads:
        load.wait()
    for j in range(9):
        if j == 4:
            continue

        @pl.when(exists(2 - j // 3, 2 - j % 3))
        def _():
            slot_copy(j).wait_recv()

    for h in range(9):
        pieces[32 * h : 32 * h + 32], pieces[288 + 32 * h : 320 + 32 * h] = two_pieces(slots_in[h])

    def plane(x, carry):
        def rows(q, carry):
            for i in range(2):
                for half in range(2):
                    y = 2 * q + i
                    total = jnp.zeros((8, 256), F32)
                    for corner in range(4):
                        at = (corner, x, pl.ds(y, 1), pl.ds(256 * half, 256))
                        k = bucket[at]
                        found = look_up(pieces, 288, k & 255, shift[at] * 32 + (k >> 8))
                        total = total + found * factor[at]
                    interp[x, pl.ds(y, 1), pl.ds(256 * half, 256)] = jnp.sum(total, axis=0, keepdims=True)
            return carry

        return lax.fori_loop(0, 4, rows, carry)

    lax.fori_loop(0, 8, plane, 0)

    pack_halos(interp, side_out, corner_out, True)
    copies = halo_copies(interp, side_out, side_in, dom_in, corner_out, corner_in, halo_send, halo_recv)
    start_all(copies)
    receive_all(rig_copies)
    unpack_halos(rigidity, rig_side_in, rig_dom_in, rig_corner_in, rig_wide)
    receive_all(copies)
    unpack_halos(interp, side_in, dom_in, corner_in, wide)

    row = lax.broadcasted_iota(jnp.int32, (16, 512), 0)
    lane = lax.broadcasted_iota(jnp.int32, (16, 512), 1)
    row_inside = ((row >= 4) | (s > 0)) & ((row < 12) | (s < slabs - 1))

    def inside(xx):
        return row_inside & ((xx >= 4) | (d > 0)) & ((xx < 12) | (d < doms - 1))

    def back_z(v):
        return jnp.where(lane == 0, 0.0, pltpu.roll(v, 1, 1))

    def ahead_z(v):
        return jnp.where(lane == 511, 0.0, pltpu.roll(v, 511, 1))

    def load_plane(xx, carry):
        here = wide[xx + 1]
        keep = inside(xx)
        at = jnp.clip(xx - 4, 0, 7)
        back = jnp.where(row == 0, side_in[0, 4, pl.ds(at, 1), :], pltpu.roll(here, 1, 0))
        ahead = jnp.where(row == 15, side_in[1, 4, pl.ds(at, 1), :], pltpu.roll(here, 15, 0))
        basis[0, 0, xx] = jnp.where(keep, COEF * (wide[xx + 2] - wide[xx]), 0.0)
        basis[0, 1, xx] = jnp.where(keep, COEF * (ahead - back), 0.0)
        basis[0, 2, xx] = jnp.where(keep, COEF * (ahead_z(here) - back_z(here)), 0.0)
        return carry

    lax.fori_loop(0, 16, load_plane, 0)

    def scaled_operate(level, c, xx):
        v = basis[level, c, xx]
        beside = basis[level, c, xx - 1] + basis[level, c, xx + 1]
        beside = beside + pltpu.roll(v, 1, 0) + pltpu.roll(v, 15, 0)
        beside = beside + back_z(v) + ahead_z(v)
        return ((rig_wide[xx + 1] + (6.0 - CENTRE)) * v - beside) * (1.0 / SPREAD)

    for level in range(1, 4):

        def next_plane(xx, carry, level=level):
            keep = inside(xx)
            for c in range(3):
                image = scaled_operate(level - 1, c, xx)
                if level > 1:
                    image = 2.0 * image - basis[level - 2, c, xx]
                basis[level, c, xx] = jnp.where(keep, image, 0.0)
            return carry

        lax.fori_loop(level, 16 - level, next_plane, 0)

    def folded(field):
        return jnp.where(low_half(field[:8]), field[8:], field[:8])

    def moment_plane(xx, totals):
        totals = list(totals)
        for c in range(3):
            w = [folded(basis[level, c, xx]) for level in range(4)]
            for level in range(4):
                centre[level, c, xx - 4] = w[level]
            w.append(folded(scaled_operate(3, c, xx)))
            pairs = ((0, 0), (0, 1), (1, 1), (1, 2), (2, 2), (2, 3), (3, 3), (3, 4))
            for i, (one, two) in enumerate(pairs):
                product = w[one] * w[two]
                product = (product[:, :128] + product[:, 128:256]) + (product[:, 256:384] + product[:, 384:])
                totals[i] = totals[i] + product
        return tuple(totals)

    totals = lax.fori_loop(4, 12, moment_plane, tuple(jnp.zeros((8, 128), F32) for _ in range(8)))
    for i in range(8):
        dom_moments[0, i : i + 1] = jnp.sum(totals[i], axis=0, keepdims=True)

    def reduce_copies(buffer, send, recv, count, device_of):
        return [
            pltpu.make_async_remote_copy(
                src_ref=buffer.at[0],
                dst_ref=buffer.at[k],
                send_sem=send.at[k],
                recv_sem=recv.at[k],
                device_id=device_of(k),
                device_id_type=MESH,
            )
            for k in range(1, count)
        ]

    dom_copies = reduce_copies(dom_moments, dom_send, dom_recv, doms, lambda k: (lax.rem(d + k, doms), s))
    slab_copies = reduce_copies(slab_moments, slab_send, slab_recv, slabs, lambda k: (d, lax.rem(s + k, slabs)))
    for copy in dom_copies:
        copy.start()

    for level in range(4):
        for c in range(3):
            for x in range(8):
                for half in range(2):
                    high, low = two_pieces(centre[level, c, x, :, 256 * half : 256 * half + 256])
                    at = 16 * x + 8 * half
                    wet_pieces[3 * level + c, at : at + 8] = high
                    wet_pieces[3 * level + c, 128 + at : 136 + at] = low

    for copy in dom_copies:
        copy.wait_recv()
    total = dom_moments[0]
    for k in range(1, doms):
        total = total + dom_moments[k]
    slab_moments[0] = total
    for copy in slab_copies:
        copy.start()

    for a in range(3):
        node = jnp.concatenate([wet_position[0, a, b : b + 1, :] for b in range(3)], axis=1)
        hot = one_hot(node & 255)
        group = (node >> 12) * 16 + ((node >> 8) & 1) * 8 + (((node >> 9) + 4) & 7)
        slot = lax.broadcasted_iota(jnp.int32, (1, 128), 1)
        live = jnp.concatenate(
            [slot < wet_tally[0:1, 3 * a + b : 3 * a + b + 1] for b in range(3)], axis=1
        )

        def gather_field(kc, carry, a=a, hot=hot, group=group, live=live):
            picked = jnp.dot(wet_pieces[kc], hot, preferred_element_type=F32)
            found = jnp.sum(pick_group(picked, 128, group), axis=0, keepdims=True)
            found = jnp.where(live, found, 0.0)
            for b in range(3):
                wet_out[3 * a + b, pl.ds(kc, 1), :] = found[:, 128 * b : 128 * b + 128]
            return carry

        lax.fori_loop(0, 12, gather_field, 0)

    wet_copies = []
    for j in range(9):
        if j == 4:
            continue
        copy = pltpu.make_async_remote_copy(
            src_ref=wet_out.at[j],
            dst_ref=wet_in.at[8 - j],
            send_sem=wet_send.at[j],
            recv_sem=wet_recv.at[8 - j],
            device_id=(d + (j // 3 - 1), s + (j % 3 - 1)),
            device_id_type=MESH,
        )
        wet_copies.append((j // 3, j % 3, copy))
    start_all(wet_copies)
    wet_in[4] = wet_out[4]

    taker = jnp.concatenate(
        [accepting[0, a, b : b + 1, :] for a in range(3) for b in range(3)], axis=1
    )
    node_row = lax.broadcasted_iota(jnp.int32, (128, 1152), 0)
    row_hot = jnp.where(node_row == (taker >> 7), 1.0, 0.0).astype(BF16)

    for copy in slab_copies:
        copy.wait_recv()
    total = slab_moments[0]
    for k in range(1, slabs):
        total = total + slab_moments[k]
    c = coefficients([jnp.sum(total[i : i + 1], axis=1, keepdims=True) for i in range(8)])

    def combine(x, carry):
        for a in range(3):
            field = c[0] * centre[0, a, x]
            for level in range(1, 4):
                field = field + c[level] * centre[level, a, x]
            disp[a, x] = half_turn(field)
        return carry

    lax.fori_loop(0, 8, combine, 0)

    receive_all(wet_copies)
    lane_of = taker & 127
    for a in range(3):
        value = jnp.concatenate(
            [
                sum(c[level] * wet_in[j, 3 * level + a : 3 * level + a + 1, :] for level in range(4))
                for j in range(9)
            ],
            axis=1,
        )
        high = value.astype(BF16).astype(F32)
        parts = [
            jnp.where(node_row == lane_of, part, 0.0).astype(BF16) for part in (high, value - high)
        ]
        spread[a] = sum(
            lax.dot_general(row_hot, part, (((1,), (1,)), ((), ())), preferred_element_type=F32)
            for part in parts
        )

    finish_all(rig_copies)
    for j in range(9):
        if j == 4:
            continue

        @pl.when(exists(j // 3, j % 3))
        def _():
            slot_copy(j).wait_send()

    finish_all(copies)
    finish_all(wet_copies)
    for copy in dom_copies + slab_copies:
        copy.wait_send()


def on_device(doms, slabs, heat, *args):
    dma = pltpu.SemaphoreType.DMA
    vm = pltpu.VMEM
    halos_out = [vm((2, 5, 8, 512), F32), vm((2, 2, 2, 8, 512), F32)]
    halos_in = [vm((2, 5, 8, 512), F32), vm((2, 5, 8, 512), F32), vm((2, 2, 2, 8, 512), F32)]
    halos = [halos_out[0], halos_in[0], halos_in[1], halos_out[1], halos_in[2]]
    whole = pl.BlockSpec(memory_space=pltpu.VMEM)
    away = pl.BlockSpec(memory_space=pl.ANY)
    disp, spread = pl.pallas_call(
        functools.partial(kernel, doms, slabs),
        out_shape=[
            jax.ShapeDtypeStruct((3, 8, 8, 512), F32),
            jax.ShapeDtypeStruct((3, 128, 128), F32),
        ],
        in_specs=[whole, whole, away, away, away, whole, whole, whole, whole],
        out_specs=[whole, whole],
        scratch_shapes=[
            vm((4, 8, 8, 512), jnp.int32),
            vm((4, 8, 8, 512), jnp.int32),
            vm((4, 8, 8, 512), F32),
            vm((128, 256), BF16),
            vm((9, 32, 256), F32),
            vm((9, 32, 256), F32),
            vm((576, 256), BF16),
            vm((8, 8, 512), F32),
            *halos,
            *halos,
            vm((18, 16, 512), F32),
            vm((18, 16, 512), F32),
            vm((4, 3, 16, 16, 512), F32),
            vm((4, 3, 8, 8, 512), F32),
            vm((doms, 8, 128), F32),
            vm((slabs, 8, 128), F32),
            vm((12, 256, 256), BF16),
            vm((9, 16, 128), F32),
            vm((9, 16, 128), F32),
            dma((3,)),
            dma((9,)),
            dma((9,)),
            dma((9,)),
            dma((9,)),
            dma((9,)),
            dma((9,)),
            dma((9,)),
            dma((9,)),
            dma((doms,)),
            dma((doms,)),
            dma((slabs,)),
            dma((slabs,)),
        ],
        compiler_params=pltpu.CompilerParams(
            collective_id=0, has_side_effects=True, vmem_limit_bytes=56 * 2**20
        ),
    )(heat.reshape(128, 128), *args)
    return disp, spread.reshape(3, -1)


def solution(mesh):
    in_specs = (
        P(BOTH),
        P(BOTH, None, None, None),
        P(None, DOM, SLAB, None),
        P(None, DOM, SLAB, None),
        P(None, DOM, SLAB, None),
        P(DOM, SLAB, None),
        P(BOTH, None, None, None),
        P(BOTH, None),
        P(BOTH, None, None, None),
    )
    out_specs = (P(None, DOM, SLAB, None), P(None, BOTH))
    return jax.shard_map(
        functools.partial(on_device, mesh.shape[DOM], mesh.shape[SLAB]),
        mesh=mesh,
        in_specs=in_specs,
        out_specs=out_specs,
        check_vma=False,
    )
```

time: 258 us -> 103 us (0.40)
  the two profiles are of different devices: /device:TPU:1 before, /device:TPU:33 now
where the time goes in v2:
time: 103 us
  Pallas kernels  96.1 us (93%)
  local copies, waits for them, and re-layouts  6.36 us (6%)
    pallas_call x1, Pallas kernels, on_device(): pl.pallas_call(functools.partial(kernel, doms, slabs), out_shape=[jax.Sha...  96.1 us
    unnamed x9, local copies, waits for them, and re-layouts  6.36 us

profile of v2, /device:TPU:33, one launch (start us, length us, event | category | flops | bytes accessed | tf_op | source)
XLA Modules:
  0.0 103.2 jit_solution(11754715784560266149)
XLA Ops:
  0.6 0.0 copy-start.1
  0.6 1.3 %copy.12.wet_position = s32[1,3,3,128]{3,2,1,0:T(4,128)} copy(s32[1,3,3,128]{3,0,2,1:T(1,128)} %param.15) | data formatting | bytes 9216 | tf_op args[6]
  1.9 0.0 copy-done.1
  1.9 0.6 copy.13.accepting
  2.5 1.9 %copy.11.emitting = s32[1,3,3,8192]{3,2,1,0:T(4,128)} copy(s32[1,3,3,8192]{3,0,2,1:T(1,128)} %param.10) | data formatting | bytes 589824 | tf_op args[1]
  4.4 96.1 %shard_map.104 = (f32[3,8,8,512]{3,2,1,0:T(8,128)}, f32[3,128,128]{2,1,0:T(8,128)}) custom-call(f32[128,128]{1,0:T(8,128)} %bitcast.7, s32[1,3,3,8192]{3,2,1,0:T(4,128)} %copy.11.emitting, s32[4,8,8,512]{3,2,1,0:T(8,128)} %shift_hbm.1, s32[4,8,8,512]{3,2,1,0:T(8,128)} %bucket_hbm.1, f32[4,8,8,512]{3,2,1,0:T(8,128)} %factor_hbm.1, f32[8,8,512]{2,1,0:T(8,128)} %rigidity.1, ...), custom_call_target="tpu_custom_call" | custom-call | tf_op jit(solution)/shard_map/pallas_call | solution.py:591
  100.6 0.0 copy-start
  100.6 1.8 %copy.16 = f32[1,3,128,128]{3,1,2,0:T(4,128)} copy(f32[1,3,128,128]{3,2,1,0:T(8,128)} %bitcast.6) | data formatting | bytes 393216
  102.4 0.0 copy-done
  102.4 0.7 copy.18
Async XLA Ops:
  0.6 1.3 %copy-start.1 = (s32[1,3,3,128]{3,0,2,1:T(1,128)S(1)}, s32[1,3,3,128]{3,0,2,1:T(1,128)}, u32[]{:S(2)}) copy-start(s32[1,3,3,128]{3,0,2,1:T(1,128)} %param.17) | copy-start | bytes 13828
  100.6 1.8 %copy-start = (f32[3,8,8,512]{3,2,1,0:T(8,128)S(1)}, f32[3,8,8,512]{3,2,1,0:T(8,128)}, u32[]{:S(2)}) copy-start(f32[3,8,8,512]{3,2,1,0:T(8,128)} %get-tuple-element.8) | copy-start | bytes 1179652

commit v3 on v2

--- a/solution.py
+++ b/solution.py
@@ -92,6 +92,19 @@
         p = [r[i] + beta * (p[i] if i < len(p) else zero) for i in range(len(r))]
         rr = new
     return x
+
+
+def gather_tree(table_rows, across, group):
+    found = [
+        jnp.take_along_axis(jnp.broadcast_to(one, (8, 128)), across, axis=1, mode="promise_in_bounds")
+        for one in table_rows
+    ]
+    bit = 0
+    while len(found) > 1:
+        odd = ((group >> bit) & 1) == 1
+        found = [jnp.where(odd, found[k + 1], found[k]) for k in range(0, len(found), 2)]
+        bit += 1
+    return found[0]
 
 
 def half_turn(tile):
@@ -307,12 +320,9 @@
     clear_blocks(slots_in)
     clear_blocks(wet_in)
     wet_out[...] = jnp.zeros(wet_out.shape, F32)
-    pl.semaphore_wait(barrier, expected)
     rig_copies = halo_copies(
         rigidity, rig_side_out, rig_side_in, rig_dom_in, rig_corner_out, rig_corner_in, rig_send, rig_recv
     )
-    start_all(rig_copies)
-
     def slot_copy(j):
         return pltpu.make_async_remote_copy(
             src_ref=slots_out.at[j],
@@ -323,28 +333,37 @@
             device_id_type=MESH,
         )
 
+    def start_slot(j):
+        @pl.when((j != 4) & exists(j // 3, lax.rem(j, 3)))
+        def _():
+            slot_copy(j).start()
+
     def slot_block(t, carry):
         j = lax.rem(t + 5, 9)
-        a, b = j // 3, lax.rem(j, 3)
-
-        def chunk(q, carry):
-            for i in range(16):
-                at = pl.multiple_of(4096 * q + 256 * i, 256)
-                k = emitting[0, a, pl.ds(b, 1), pl.ds(at, 256)]
-                across = (k >> 13) * 128 + (k & 127)
-                found = look_up(heat_pieces, 64, across, (k >> 7) & 63)
-                slots_out[j, pl.ds(16 * q + i, 1), :] = jnp.sum(found, axis=0, keepdims=True)
-            return carry
-
-        lax.fori_loop(0, 2, chunk, 0)
-
-        @pl.when((j != 4) & exists(a, b))
+        for i in range(16):
+            k = jnp.concatenate([emitting[pl.ds(64 * j + 2 * i + r, 1), :] for r in range(2)], axis=1)
+            across = (k >> 13) * 128 + (k & 127)
+            found = look_up(heat_pieces, 64, across, (k >> 7) & 63)
+            found = jnp.sum(found, axis=0, keepdims=True)
+            slots_out[j, 2 * i : 2 * i + 1] = found[:, :128]
+            slots_out[j, 2 * i + 1 : 2 * i + 2] = found[:, 128:]
+        for i in range(4, 8):
+            k = emitting[pl.ds(pl.multiple_of(64 * j + 8 * i, 8), 8), :]
+            slots_out[j, 8 * i : 8 * i + 8] = gather_tree([heat[r : r + 1] for r in range(128)], k & 127, k >> 7)
+
+        @pl.when(t == 1)
         def _():
-            slot_copy(j).start()
+            pl.semaphore_wait(barrier, expected)
+            start_slot(5)
+
+        @pl.when(t >= 1)
+        def _():
+            start_slot(j)
 
         return carry
 
     lax.fori_loop(0, 9, slot_block, 0)
+    start_all(rig_copies)
     slots_in[4] = slots_out[4]
     for load in loads:
         load.wait()
@@ -357,23 +376,46 @@
             slot_copy(j).wait_recv()
 
     for h in range(9):
-        pieces[32 * h : 32 * h + 32], pieces[288 + 32 * h : 320 + 32 * h] = two_pieces(slots_in[h])
+        table = jnp.concatenate([slots_in[h, :32], slots_in[h, 32:]], axis=1)
+        pieces[32 * h : 32 * h + 32], pieces[288 + 32 * h : 320 + 32 * h] = two_pieces(table)
+
+    def matched(k, holder):
+        return look_up(pieces, 288, ((k >> 12) & 1) * 128 + (k & 127), holder * 32 + ((k >> 7) & 31))
 
     def plane(x, carry):
-        def rows(q, carry):
-            for i in range(2):
-                for half in range(2):
-                    y = 2 * q + i
+        def rows(half_plane, last):
+            for u in range(2):
+                q = 2 * half_plane + u
+
+                def pair(ref, corner):
+                    ends = [ref[corner, x, pl.ds(2 * q + i, 1), pl.ds(256, 256)] for i in range(2)]
+                    return jnp.concatenate([end[:, :128] for end in ends], axis=1)
+
+                for i in range(2):
                     total = jnp.zeros((8, 256), F32)
                     for corner in range(4):
-                        at = (corner, x, pl.ds(y, 1), pl.ds(256 * half, 256))
-                        k = bucket[at]
-                        found = look_up(pieces, 288, k & 255, shift[at] * 32 + (k >> 8))
-                        total = total + found * factor[at]
-                    interp[x, pl.ds(y, 1), pl.ds(256 * half, 256)] = jnp.sum(total, axis=0, keepdims=True)
-            return carry
-
-        return lax.fori_loop(0, 4, rows, carry)
+                        at = (corner, x, pl.ds(2 * q + i, 1), pl.ds(0, 256))
+                        total = total + matched(bucket[at], shift[at]) * factor[at]
+                    interp[x, pl.ds(2 * q + i, 1), pl.ds(0, 256)] = jnp.sum(total, axis=0, keepdims=True)
+                total = jnp.zeros((8, 256), F32)
+                for corner in range(4):
+                    total = total + matched(pair(bucket, corner), pair(shift, corner)) * pair(factor, corner)
+                total = jnp.sum(total, axis=0, keepdims=True)
+                for i in range(2):
+                    both = jnp.concatenate([total[:, 128 * i : 128 * i + 128]] * 2, axis=1)
+                    interp[x, pl.ds(2 * q + i, 1), pl.ds(256, 256)] = both
+
+                at = (q, x, slice(None), pl.ds(384, 128))
+                k, holder = bucket[at], shift[at]
+                found = None
+                for h in range(9):
+                    one = gather_tree([slots_in[h, r : r + 1] for r in range(64)], k & 127, k >> 7)
+                    found = one if found is None else jnp.where(holder == h, one, found)
+                last = last + factor[at] * found
+            return last
+
+        interp[x, :, 384:512] = lax.fori_loop(0, 2, rows, jnp.zeros((8, 128), F32))
+        return carry
 
     lax.fori_loop(0, 8, plane, 0)
 
@@ -452,23 +494,22 @@
     for i in range(8):
         dom_moments[0, i : i + 1] = jnp.sum(totals[i], axis=0, keepdims=True)
 
-    def reduce_copies(buffer, send, recv, count, device_of):
-        return [
-            pltpu.make_async_remote_copy(
-                src_ref=buffer.at[0],
-                dst_ref=buffer.at[k],
-                send_sem=send.at[k],
-                recv_sem=recv.at[k],
-                device_id=device_of(k),
-                device_id_type=MESH,
-            )
-            for k in range(1, count)
-        ]
-
-    dom_copies = reduce_copies(dom_moments, dom_send, dom_recv, doms, lambda k: (lax.rem(d + k, doms), s))
-    slab_copies = reduce_copies(slab_moments, slab_send, slab_recv, slabs, lambda k: (d, lax.rem(s + k, slabs)))
-    for copy in dom_copies:
-        copy.start()
+    def reduce_copy(buffer, send, recv, source, target, device):
+        return pltpu.make_async_remote_copy(
+            src_ref=buffer.at[source],
+            dst_ref=buffer.at[target],
+            send_sem=send,
+            recv_sem=recv,
+            device_id=device,
+            device_id_type=MESH,
+        )
+
+    for k in range(1, doms):
+        reduce_copy(dom_moments, dom_send, dom_recv, 0, k, (lax.rem(d + k, doms), s)).start()
+    others = pl.ds(1, doms - 1)
+    dom_all = reduce_copy(dom_moments, dom_send, dom_recv, others, others, (lax.rem(d + 1, doms), s))
+    others = pl.ds(1, slabs - 1)
+    slab_all = reduce_copy(slab_moments, slab_send, slab_recv, others, others, (d, lax.rem(s + 1, slabs)))
 
     for level in range(4):
         for c in range(3):
@@ -476,36 +517,35 @@
                 for half in range(2):
                     high, low = two_pieces(centre[level, c, x, :, 256 * half : 256 * half + 256])
                     at = 16 * x + 8 * half
-                    wet_pieces[3 * level + c, at : at + 8] = high
-                    wet_pieces[3 * level + c, 128 + at : 136 + at] = low
-
-    for copy in dom_copies:
-        copy.wait_recv()
-    total = dom_moments[0]
-    for k in range(1, doms):
-        total = total + dom_moments[k]
-    slab_moments[0] = total
-    for copy in slab_copies:
-        copy.start()
-
-    for a in range(3):
-        node = jnp.concatenate([wet_position[0, a, b : b + 1, :] for b in range(3)], axis=1)
-        hot = one_hot(node & 255)
+                    at = at + 256 * (3 * level + c)
+                    wet_pieces[at : at + 8] = high
+                    wet_pieces[128 + at : 136 + at] = low
+
+    def wet_block(a):
+        node = jnp.concatenate([wet_position[3 * a + b] for b in range(3)], axis=1)
         group = (node >> 12) * 16 + ((node >> 8) & 1) * 8 + (((node >> 9) + 4) & 7)
         slot = lax.broadcasted_iota(jnp.int32, (1, 128), 1)
         live = jnp.concatenate(
             [slot < wet_tally[0:1, 3 * a + b : 3 * a + b + 1] for b in range(3)], axis=1
         )
-
-        def gather_field(kc, carry, a=a, hot=hot, group=group, live=live):
-            picked = jnp.dot(wet_pieces[kc], hot, preferred_element_type=F32)
-            found = jnp.sum(pick_group(picked, 128, group), axis=0, keepdims=True)
-            found = jnp.where(live, found, 0.0)
+        picked = jnp.dot(wet_pieces[...], one_hot(node & 255), preferred_element_type=F32)
+        for kc in range(12):
+            found = pick_group(picked[256 * kc : 256 * kc + 256], 128, group)
+            found = jnp.where(live, jnp.sum(found, axis=0, keepdims=True), 0.0)
+            at = kc // 3 * 4 + kc % 3
             for b in range(3):
-                wet_out[3 * a + b, pl.ds(kc, 1), :] = found[:, 128 * b : 128 * b + 128]
-            return carry
-
-        lax.fori_loop(0, 12, gather_field, 0)
+                wet_out[3 * a + b, at : at + 1] = found[:, 128 * b : 128 * b + 128]
+
+    wet_block(0)
+    dom_all.wait_recv()
+    total = dom_moments[0]
+    for k in range(1, doms):
+        total = total + dom_moments[k]
+    slab_moments[0] = total
+    for k in range(1, slabs):
+        reduce_copy(slab_moments, slab_send, slab_recv, 0, k, (d, lax.rem(s + k, slabs))).start()
+    wet_block(1)
+    wet_block(2)
 
     wet_copies = []
     for j in range(9):
@@ -523,14 +563,11 @@
     start_all(wet_copies)
     wet_in[4] = wet_out[4]
 
-    taker = jnp.concatenate(
-        [accepting[0, a, b : b + 1, :] for a in range(3) for b in range(3)], axis=1
-    )
-    node_row = lax.broadcasted_iota(jnp.int32, (128, 1152), 0)
-    row_hot = jnp.where(node_row == (taker >> 7), 1.0, 0.0).astype(BF16)
-
-    for copy in slab_copies:
-        copy.wait_recv()
+    taker = jnp.concatenate([accepting[j] for j in range(9)], axis=1)
+    lane_of = lax.broadcasted_iota(jnp.int32, (128, 1152), 0)
+    lane_hot = jnp.where(lane_of == (taker & 127), 1.0, 0.0).astype(BF16)
+
+    slab_all.wait_recv()
     total = slab_moments[0]
     for k in range(1, slabs):
         total = total + slab_moments[k]
@@ -547,23 +584,22 @@
     lax.fori_loop(0, 8, combine, 0)
 
     receive_all(wet_copies)
-    lane_of = taker & 127
-    for a in range(3):
-        value = jnp.concatenate(
-            [
-                sum(c[level] * wet_in[j, 3 * level + a : 3 * level + a + 1, :] for level in range(4))
-                for j in range(9)
-            ],
-            axis=1,
+    sub = lax.broadcasted_iota(jnp.int32, (8, 1), 0)
+    first = jnp.where(sub < 4, c[0], c[1])
+    second = jnp.where(sub < 4, c[2], c[3])
+    value = jnp.concatenate([wet_in[j, :8] * first + wet_in[j, 8:] * second for j in range(9)], axis=1)
+    value = value + half_turn(value)
+    high = value.astype(BF16).astype(F32)
+    apart = (taker >> 7) - (lax.broadcasted_iota(jnp.int32, (8, 1152), 0) >> 2)
+    for part_of in range(4):
+        at = range(16 * part_of, 16 * part_of + 16)
+        lines = [
+            jnp.where(apart == 2 * h, part, 0.0).astype(BF16) for part in (high, value - high) for h in at
+        ]
+        put = lax.dot_general(
+            jnp.concatenate(lines, axis=0), lane_hot, (((1,), (1,)), ((), ())), preferred_element_type=F32
         )
-        high = value.astype(BF16).astype(F32)
-        parts = [
-            jnp.where(node_row == lane_of, part, 0.0).astype(BF16) for part in (high, value - high)
-        ]
-        spread[a] = sum(
-            lax.dot_general(row_hot, part, (((1,), (1,)), ((), ())), preferred_element_type=F32)
-            for part in parts
-        )
+        spread[128 * part_of : 128 * part_of + 128] = put[:128] + put[128:]
 
     finish_all(rig_copies)
     for j in range(9):
@@ -576,11 +612,11 @@
 
     finish_all(copies)
     finish_all(wet_copies)
-    for copy in dom_copies + slab_copies:
-        copy.wait_send()
-
-
-def on_device(doms, slabs, heat, *args):
+    dom_all.wait_send()
+    slab_all.wait_send()
+
+
+def on_device(doms, slabs, heat, emitting, shift, bucket, factor, rigidity, position, tally, accepting):
     dma = pltpu.SemaphoreType.DMA
     vm = pltpu.VMEM
     halos_out = [vm((2, 5, 8, 512), F32), vm((2, 2, 2, 8, 512), F32)]
@@ -592,7 +628,7 @@
         functools.partial(kernel, doms, slabs),
         out_shape=[
             jax.ShapeDtypeStruct((3, 8, 8, 512), F32),
-            jax.ShapeDtypeStruct((3, 128, 128), F32),
+            jax.ShapeDtypeStruct((512, 128), F32),
         ],
         in_specs=[whole, whole, away, away, away, whole, whole, whole, whole],
         out_specs=[whole, whole],
@@ -601,8 +637,8 @@
             vm((4, 8, 8, 512), jnp.int32),
             vm((4, 8, 8, 512), F32),
             vm((128, 256), BF16),
-            vm((9, 32, 256), F32),
-            vm((9, 32, 256), F32),
+            vm((9, 64, 128), F32),
+            vm((9, 64, 128), F32),
             vm((576, 256), BF16),
             vm((8, 8, 512), F32),
             *halos,
@@ -613,7 +649,7 @@
             vm((4, 3, 8, 8, 512), F32),
             vm((doms, 8, 128), F32),
             vm((slabs, 8, 128), F32),
-            vm((12, 256, 256), BF16),
+            vm((3072, 256), BF16),
             vm((9, 16, 128), F32),
             vm((9, 16, 128), F32),
             dma((3,)),
@@ -625,16 +661,27 @@
             dma((9,)),
             dma((9,)),
             dma((9,)),
-            dma((doms,)),
-            dma((doms,)),
-            dma((slabs,)),
-            dma((slabs,)),
+            dma,
+            dma,
+            dma,
+            dma,
         ],
         compiler_params=pltpu.CompilerParams(
             collective_id=0, has_side_effects=True, vmem_limit_bytes=56 * 2**20
         ),
-    )(heat.reshape(128, 128), *args)
-    return disp, spread.reshape(3, -1)
+    )(
+        heat.reshape(128, 128),
+        emitting.reshape(576, 128),
+        shift,
+        bucket,
+        factor,
+        rigidity,
+        position.reshape(9, 1, 128),
+        tally,
+        accepting.reshape(9, 1, 128),
+    )
+    spread = spread.reshape(128, 4, 128)[:, :3]
+    return disp, spread.transpose(1, 0, 2).reshape(3, -1)
 
 
 def solution(mesh):

time: 103 us -> 78.4 us (0.76)
  the two profiles are of different devices: /device:TPU:33 before, /device:TPU:1 now
where the time goes in v3:
time: 78.4 us; the launch traced here: 78.1 us
  Pallas kernels  75 us (96%)
  local copies, waits for them, and re-layouts  2.47 us (3%)
    pallas_call x1, Pallas kernels, on_device(): pl.pallas_call(functools.partial(kernel, doms, slabs), out_shape=[jax.Sha...  75 us
    reshape x1, local copies, waits for them, and re-layouts, on_device(): return (disp, spread.transpose(1, 0, 2).reshape(3, -1))  1.72 us

profile of v3, /device:TPU:1, one launch (start us, length us, event | category | flops | bytes accessed | tf_op | source)
XLA Modules:
  0.0 78.1 jit_solution(11611929179881162019)
XLA Ops:
  0.6 75.0 %shard_map.104 = (f32[3,8,8,512]{3,2,1,0:T(8,128)}, f32[512,128]{1,0:T(8,128)}) custom-call(f32[128,128]{1,0:T(8,128)} %bitcast.11, s32[576,128]{1,0:T(8,128)} %bitcast.9, s32[4,8,8,512]{3,2,1,0:T(8,128)} %shift_hbm.1, s32[4,8,8,512]{3,2,1,0:T(8,128)} %bucket_hbm.1, f32[4,8,8,512]{3,2,1,0:T(8,128)} %factor_hbm.1, f32[8,8,512]{2,1,0:T(8,128)} %rigidity.1, ...), custom_call_target="tpu_custom_call" | custom-call | tf_op jit(solution)/shard_map/pallas_call | solution.py:627
  75.6 0.0 copy-start
  75.6 1.7 %slice_bitcast_fusion = f32[3,16384]{1,0:T(4,128)} fusion(f32[128,4,128]{2,1,0:T(4,128)} %bitcast.10), kind=kLoop, calls=%fused_computation | loop fusion | bytes 393216 | tf_op jit(solution)/shard_map/reshape | solution.py:684
  77.4 0.0 copy-done
  77.4 0.7 copy.13
Async XLA Ops:
  75.6 1.7 %copy-start = (f32[3,8,8,512]{3,2,1,0:T(8,128)S(1)}, f32[3,8,8,512]{3,2,1,0:T(8,128)}, u32[]{:S(2)}) copy-start(f32[3,8,8,512]{3,2,1,0:T(8,128)} %get-tuple-element.8) | copy-start | bytes 1179652

commit v4 on v3

--- a/solution.py
+++ b/solution.py
@@ -115,20 +115,19 @@
     return lax.broadcasted_iota(jnp.int32, tile.shape, 0) < 4
 
 
-def pack_halos(block, side, corner, fifth):
+def pack_pair(near, far):
+    return (
+        jnp.where(low_half(near), near, half_turn(far)),
+        jnp.where(low_half(near), half_turn(near), far),
+    )
+
+
+def pack_halos(block, side, corner):
     for x in range(4):
-        near, far = block[x], block[x + 4]
-        side[0, x] = jnp.where(low_half(near), near, half_turn(far))
-        side[1, x] = jnp.where(low_half(near), half_turn(near), far)
-    if fifth:
-        for x in range(8):
-            side[0, 4, x : x + 1] = block[x, 4:5]
-            side[1, 4, x : x + 1] = block[x, 3:4]
+        side[0, x], side[1, x] = pack_pair(block[x], block[x + 4])
     for a in range(2):
         for j in range(2):
-            near, far = block[4 * a + j], block[4 * a + 2 + j]
-            corner[a, 0, j] = jnp.where(low_half(near), near, half_turn(far))
-            corner[a, 1, j] = jnp.where(low_half(near), half_turn(near), far)
+            corner[a, 0, j], corner[a, 1, j] = pack_pair(block[4 * a + j], block[4 * a + 2 + j])
 
 
 def unpack_halos(block, side, dom, corner, wide):
@@ -192,7 +191,10 @@
     rig_corner_in,
     wide,
     rig_wide,
-    basis,
+    basis_0,
+    basis_1,
+    basis_2,
+    basis_3,
     centre,
     dom_moments,
     slab_moments,
@@ -312,9 +314,6 @@
                 blocks[j] = jnp.zeros(blocks.shape[1:], F32)
 
     heat_pieces[:64], heat_pieces[64:] = two_pieces(jnp.concatenate([heat[:64], heat[64:]], axis=1))
-    pack_halos(rigidity, rig_side_out, rig_corner_out, False)
-    for b in range(2):
-        rig_side_out[b, 4] = jnp.zeros((8, 512), F32)
     clear_missing(rig_side_in, rig_dom_in, rig_corner_in)
     clear_missing(side_in, dom_in, corner_in)
     clear_blocks(slots_in)
@@ -351,18 +350,22 @@
             k = emitting[pl.ds(pl.multiple_of(64 * j + 8 * i, 8), 8), :]
             slots_out[j, 8 * i : 8 * i + 8] = gather_tree([heat[r : r + 1] for r in range(128)], k & 127, k >> 7)
 
-        @pl.when(t == 1)
+        @pl.when(t == 3)
         def _():
             pl.semaphore_wait(barrier, expected)
-            start_slot(5)
-
-        @pl.when(t >= 1)
+            for early in (5, 6, 7):
+                start_slot(jnp.int32(early))
+
+        @pl.when(t >= 3)
         def _():
             start_slot(j)
 
         return carry
 
     lax.fori_loop(0, 9, slot_block, 0)
+    pack_halos(rigidity, rig_side_out, rig_corner_out)
+    for b in range(2):
+        rig_side_out[b, 4] = jnp.zeros((8, 512), F32)
     start_all(rig_copies)
     slots_in[4] = slots_out[4]
     for load in loads:
@@ -417,11 +420,57 @@
         interp[x, :, 384:512] = lax.fori_loop(0, 2, rows, jnp.zeros((8, 128), F32))
         return carry
 
-    lax.fori_loop(0, 8, plane, 0)
-
-    pack_halos(interp, side_out, corner_out, True)
     copies = halo_copies(interp, side_out, side_in, dom_in, corner_out, corner_in, halo_send, halo_recv)
-    start_all(copies)
+
+    def send_piece(a, b, src, dst):
+        j = 3 * a + b
+
+        @pl.when(exists(a, b))
+        def _():
+            pltpu.make_async_remote_copy(
+                src_ref=src,
+                dst_ref=dst,
+                send_sem=halo_send.at[j],
+                recv_sem=halo_recv.at[8 - j],
+                device_id=(d + (a - 1), s + (b - 1)),
+                device_id_type=MESH,
+            ).start()
+
+    def plane_pair(q, carry):
+        p = lax.rem(2 * q, 4) + q // 2
+        lax.fori_loop(0, 2, lambda e, carry: plane(p + 4 * e, carry), 0)
+        near, far = interp[p], interp[p + 4]
+        side_out[0, p], side_out[1, p] = pack_pair(near, far)
+        for b in range(2):
+            side_out[b, 4, pl.ds(p, 1), :] = near[4 - b : 5 - b]
+            side_out[b, 4, pl.ds(p + 4, 1), :] = far[4 - b : 5 - b]
+            send_piece(1, 2 * b, side_out.at[b, p], side_in.at[1 - b, p])
+        send_piece(0, 1, interp.at[p], dom_in.at[1, p])
+        send_piece(2, 1, interp.at[p + 4], dom_in.at[0, p + 1])
+
+        @pl.when(q == 0)
+        def _():
+            send_piece(0, 1, interp.at[4], dom_in.at[1, 4])
+
+        @pl.when(q % 2 == 1)
+        def _():
+            j = q // 2
+            for a in range(2):
+                pieces_of = pack_pair(interp[4 * a + j], interp[4 * a + 2 + j])
+                for b in range(2):
+                    corner_out[a, b, j] = pieces_of[b]
+                    send_piece(2 * a, 2 * b, corner_out.at[a, b, j], corner_in.at[1 - a, 1 - b, j])
+
+        @pl.when(q == 3)
+        def _():
+            send_piece(2, 1, interp.at[3], dom_in.at[0, 0])
+            for b in range(2):
+                send_piece(1, 2 * b, side_out.at[b, 4], side_in.at[1 - b, 4])
+
+        return carry
+
+    lax.fori_loop(0, 4, plane_pair, 0)
+
     receive_all(rig_copies)
     unpack_halos(rigidity, rig_side_in, rig_dom_in, rig_corner_in, rig_wide)
     receive_all(copies)
@@ -439,6 +488,14 @@
 
     def ahead_z(v):
         return jnp.where(lane == 511, 0.0, pltpu.roll(v, 511, 1))
+
+    basis = (basis_0, basis_1, basis_2, basis_3)
+
+    def by_twos(first, end, body, carry):
+        def two(i, carry):
+            return body(first + 2 * i + 1, body(first + 2 * i, carry))
+
+        return lax.fori_loop(0, (end - first) // 2, two, carry)
 
     def load_plane(xx, carry):
         here = wide[xx + 1]
@@ -446,16 +503,16 @@
         at = jnp.clip(xx - 4, 0, 7)
         back = jnp.where(row == 0, side_in[0, 4, pl.ds(at, 1), :], pltpu.roll(here, 1, 0))
         ahead = jnp.where(row == 15, side_in[1, 4, pl.ds(at, 1), :], pltpu.roll(here, 15, 0))
-        basis[0, 0, xx] = jnp.where(keep, COEF * (wide[xx + 2] - wide[xx]), 0.0)
-        basis[0, 1, xx] = jnp.where(keep, COEF * (ahead - back), 0.0)
-        basis[0, 2, xx] = jnp.where(keep, COEF * (ahead_z(here) - back_z(here)), 0.0)
+        basis_0[0, xx] = jnp.where(keep, COEF * (wide[xx + 2] - wide[xx]), 0.0)
+        basis_0[1, xx] = jnp.where(keep, COEF * (ahead - back), 0.0)
+        basis_0[2, xx] = jnp.where(keep, COEF * (ahead_z(here) - back_z(here)), 0.0)
         return carry
 
-    lax.fori_loop(0, 16, load_plane, 0)
+    by_twos(0, 16, load_plane, 0)
 
     def scaled_operate(level, c, xx):
-        v = basis[level, c, xx]
-        beside = basis[level, c, xx - 1] + basis[level, c, xx + 1]
+        v = basis[level][c, xx]
+        beside = basis[level][c, xx - 1] + basis[level][c, xx + 1]
         beside = beside + pltpu.roll(v, 1, 0) + pltpu.roll(v, 15, 0)
         beside = beside + back_z(v) + ahead_z(v)
         return ((rig_wide[xx + 1] + (6.0 - CENTRE)) * v - beside) * (1.0 / SPREAD)
@@ -467,11 +524,11 @@
             for c in range(3):
                 image = scaled_operate(level - 1, c, xx)
                 if level > 1:
-                    image = 2.0 * image - basis[level - 2, c, xx]
-                basis[level, c, xx] = jnp.where(keep, image, 0.0)
+                    image = 2.0 * image - basis[level - 2][c, xx]
+                basis[level][c, xx] = jnp.where(keep, image, 0.0)
             return carry
 
-        lax.fori_loop(level, 16 - level, next_plane, 0)
+        by_twos(level, 16 - level, next_plane, 0)
 
     def folded(field):
         return jnp.where(low_half(field[:8]), field[8:], field[:8])
@@ -479,7 +536,7 @@
     def moment_plane(xx, totals):
         totals = list(totals)
         for c in range(3):
-            w = [folded(basis[level, c, xx]) for level in range(4)]
+            w = [folded(basis[level][c, xx]) for level in range(4)]
             for level in range(4):
                 centre[level, c, xx - 4] = w[level]
             w.append(folded(scaled_operate(3, c, xx)))
@@ -490,7 +547,7 @@
                 totals[i] = totals[i] + product
         return tuple(totals)
 
-    totals = lax.fori_loop(4, 12, moment_plane, tuple(jnp.zeros((8, 128), F32) for _ in range(8)))
+    totals = by_twos(4, 12, moment_plane, tuple(jnp.zeros((8, 128), F32) for _ in range(8)))
     for i in range(8):
         dom_moments[0, i : i + 1] = jnp.sum(totals[i], axis=0, keepdims=True)
 
@@ -599,7 +656,9 @@
         put = lax.dot_general(
             jnp.concatenate(lines, axis=0), lane_hot, (((1,), (1,)), ((), ())), preferred_element_type=F32
         )
-        spread[128 * part_of : 128 * part_of + 128] = put[:128] + put[128:]
+        put = put[:128] + put[128:]
+        for h in range(32):
+            spread[:, 4096 * part_of + 128 * h : 4096 * part_of + 128 * h + 128] = put[4 * h : 4 * h + 3]
 
     finish_all(rig_copies)
     for j in range(9):
@@ -624,11 +683,11 @@
     halos = [halos_out[0], halos_in[0], halos_in[1], halos_out[1], halos_in[2]]
     whole = pl.BlockSpec(memory_space=pltpu.VMEM)
     away = pl.BlockSpec(memory_space=pl.ANY)
-    disp, spread = pl.pallas_call(
+    return pl.pallas_call(
         functools.partial(kernel, doms, slabs),
         out_shape=[
             jax.ShapeDtypeStruct((3, 8, 8, 512), F32),
-            jax.ShapeDtypeStruct((512, 128), F32),
+            jax.ShapeDtypeStruct((3, 16384), F32),
         ],
         in_specs=[whole, whole, away, away, away, whole, whole, whole, whole],
         out_specs=[whole, whole],
@@ -645,7 +704,7 @@
             *halos,
             vm((18, 16, 512), F32),
             vm((18, 16, 512), F32),
-            vm((4, 3, 16, 16, 512), F32),
+            *[vm((3, 16, 16, 512), F32) for _ in range(4)],
             vm((4, 3, 8, 8, 512), F32),
             vm((doms, 8, 128), F32),
             vm((slabs, 8, 128), F32),
@@ -680,8 +739,6 @@
         tally,
         accepting.reshape(9, 1, 128),
     )
-    spread = spread.reshape(128, 4, 128)[:, :3]
-    return disp, spread.transpose(1, 0, 2).reshape(3, -1)
 
 
 def solution(mesh):

time: 78.4 us -> 74.5 us (0.950)
  Pallas kernels: 75 us -> 71.1 us
    pallas_call x1, Pallas kernels: 75 us -> 71.1 us  [on_device(): pl.pallas_call(functools.partial(kernel, doms, slabs), out_shape=[jax.Sha...]
    unnamed x3 -> x4, local copies, waits for them, and re-layouts: 0.75 us -> 2.52 us
    reshape x1 -> x0, local copies, waits for them, and re-layouts: 1.72 us -> none  [on_device(): return (disp, spread.transpose(1, 0, 2).reshape(3, -1))]
where the time goes in v4:
time: 74.5 us; the launch traced here: 74.3 us
  Pallas kernels  71.1 us (95%)
  local copies, waits for them, and re-layouts  2.52 us (3%)
    pallas_call x1, Pallas kernels, on_device(): pl.pallas_call(functools.partial(kernel, doms, slabs), out_shape=[jax.Sha...  71.1 us
    unnamed x4, local copies, waits for them, and re-layouts  2.52 us

profile of v4, /device:TPU:1, one launch (start us, length us, event | category | flops | bytes accessed | tf_op | source)
XLA Modules:
  0.0 74.3 jit_solution(2334657223137586934)
XLA Ops:
  0.6 71.1 %shard_map.104 = (f32[3,8,8,512]{3,2,1,0:T(8,128)}, f32[3,16384]{1,0:T(4,128)}) custom-call(f32[128,128]{1,0:T(8,128)} %bitcast.5, s32[576,128]{1,0:T(8,128)} %bitcast.4, s32[4,8,8,512]{3,2,1,0:T(8,128)} %shift_hbm.1, s32[4,8,8,512]{3,2,1,0:T(8,128)} %bucket_hbm.1, f32[4,8,8,512]{3,2,1,0:T(8,128)} %factor_hbm.1, f32[8,8,512]{2,1,0:T(8,128)} %rigidity.1, ...), custom_call_target="tpu_custom_call" | custom-call | tf_op jit(solution)/shard_map/pallas_call | solution.py:686
  71.8 0.0 copy-start
  71.8 1.8 %copy.13 = f32[3,8,8,512]{3,2,1,0:T(8,128)} copy(f32[3,8,8,512]{3,2,1,0:T(8,128)} %get-tuple-element.4) | data formatting | bytes 786432
  73.6 0.0 copy-done
  73.6 0.7 copy.14
Async XLA Ops:
  71.8 1.8 %copy-start = (f32[3,16384]{1,0:T(4,128)S(1)}, f32[3,16384]{1,0:T(4,128)}, u32[]{:S(2)}) copy-start(f32[3,16384]{1,0:T(4,128)} %get-tuple-element.5) | copy-start | bytes 589828

commit v5 on v4

--- a/solution.py
+++ b/solution.py
@@ -491,11 +491,13 @@
 
     basis = (basis_0, basis_1, basis_2, basis_3)
 
-    def by_twos(first, end, body, carry):
-        def two(i, carry):
-            return body(first + 2 * i + 1, body(first + 2 * i, carry))
-
-        return lax.fori_loop(0, (end - first) // 2, two, carry)
+    def in_groups(first, end, size, body, carry):
+        def group(i, carry):
+            for k in range(size):
+                carry = body(first + size * i + k, carry)
+            return carry
+
+        return lax.fori_loop(0, (end - first) // size, group, carry)
 
     def load_plane(xx, carry):
         here = wide[xx + 1]
@@ -508,7 +510,7 @@
         basis_0[2, xx] = jnp.where(keep, COEF * (ahead_z(here) - back_z(here)), 0.0)
         return carry
 
-    by_twos(0, 16, load_plane, 0)
+    in_groups(0, 16, 4, load_plane, 0)
 
     def scaled_operate(level, c, xx):
         v = basis[level][c, xx]
@@ -528,7 +530,7 @@
                 basis[level][c, xx] = jnp.where(keep, image, 0.0)
             return carry
 
-        by_twos(level, 16 - level, next_plane, 0)
+        in_groups(level, 16 - level, (7, 4, 5)[level - 1], next_plane, 0)
 
     def folded(field):
         return jnp.where(low_half(field[:8]), field[8:], field[:8])
@@ -547,7 +549,7 @@
                 totals[i] = totals[i] + product
         return tuple(totals)
 
-    totals = by_twos(4, 12, moment_plane, tuple(jnp.zeros((8, 128), F32) for _ in range(8)))
+    totals = in_groups(4, 12, 4, moment_plane, tuple(jnp.zeros((8, 128), F32) for _ in range(8)))
     for i in range(8):
         dom_moments[0, i : i + 1] = jnp.sum(totals[i], axis=0, keepdims=True)
 

time: 74.5 us -> 73.3 us (0.984)
  Pallas kernels: 71.1 us -> 70 us
    pallas_call x1, Pallas kernels: 71.1 us -> 70 us  [on_device(): pl.pallas_call(functools.partial(kernel, doms, slabs), out_shape=[jax.Sha...]
where the time goes in v5:
time: 73.3 us; the launch traced here: 73.2 us
  Pallas kernels  70 us (95%)
  local copies, waits for them, and re-layouts  2.52 us (3%)
    pallas_call x1, Pallas kernels, on_device(): pl.pallas_call(functools.partial(kernel, doms, slabs), out_shape=[jax.Sha...  70 us
    unnamed x4, local copies, waits for them, and re-layouts  2.52 us

profile of v5, /device:TPU:1, one launch (start us, length us, event | category | flops | bytes accessed | tf_op | source)
XLA Modules:
  0.0 73.2 jit_solution(15943741691418745457)
XLA Ops:
  0.6 70.0 %shard_map.104 = (f32[3,8,8,512]{3,2,1,0:T(8,128)}, f32[3,16384]{1,0:T(4,128)}) custom-call(f32[128,128]{1,0:T(8,128)} %bitcast.5, s32[576,128]{1,0:T(8,128)} %bitcast.4, s32[4,8,8,512]{3,2,1,0:T(8,128)} %shift_hbm.1, s32[4,8,8,512]{3,2,1,0:T(8,128)} %bucket_hbm.1, f32[4,8,8,512]{3,2,1,0:T(8,128)} %factor_hbm.1, f32[8,8,512]{2,1,0:T(8,128)} %rigidity.1, ...), custom_call_target="tpu_custom_call" | custom-call | tf_op jit(solution)/shard_map/pallas_call | solution.py:688
  70.6 0.0 copy-start
  70.7 1.8 %copy.13 = f32[3,8,8,512]{3,2,1,0:T(8,128)} copy(f32[3,8,8,512]{3,2,1,0:T(8,128)} %get-tuple-element.4) | data formatting | bytes 786432
  72.5 0.0 copy-done
  72.5 0.7 copy.14
Async XLA Ops:
  70.6 1.8 %copy-start = (f32[3,16384]{1,0:T(4,128)S(1)}, f32[3,16384]{1,0:T(4,128)}, u32[]{:S(2)}) copy-start(f32[3,16384]{1,0:T(4,128)} %get-tuple-element.5) | copy-start | bytes 589828

commit v6 on v5

--- a/solution.py
+++ b/solution.py
@@ -595,17 +595,6 @@
             for b in range(3):
                 wet_out[3 * a + b, at : at + 1] = found[:, 128 * b : 128 * b + 128]
 
-    wet_block(0)
-    dom_all.wait_recv()
-    total = dom_moments[0]
-    for k in range(1, doms):
-        total = total + dom_moments[k]
-    slab_moments[0] = total
-    for k in range(1, slabs):
-        reduce_copy(slab_moments, slab_send, slab_recv, 0, k, (d, lax.rem(s + k, slabs))).start()
-    wet_block(1)
-    wet_block(2)
-
     wet_copies = []
     for j in range(9):
         if j == 4:
@@ -619,7 +608,21 @@
             device_id_type=MESH,
         )
         wet_copies.append((j // 3, j % 3, copy))
-    start_all(wet_copies)
+
+    def wet_row(a):
+        wet_block(a)
+        start_all([one for one in wet_copies if one[0] == a])
+
+    wet_row(0)
+    dom_all.wait_recv()
+    total = dom_moments[0]
+    for k in range(1, doms):
+        total = total + dom_moments[k]
+    slab_moments[0] = total
+    for k in range(1, slabs):
+        reduce_copy(slab_moments, slab_send, slab_recv, 0, k, (d, lax.rem(s + k, slabs))).start()
+    wet_row(2)
+    wet_row(1)
     wet_in[4] = wet_out[4]
 
     taker = jnp.concatenate([accepting[j] for j in range(9)], axis=1)

time: 73.3 us -> 73.3 us (level)
  no operation moved by 1% of the time
where the time goes in v6:
time: 73.3 us; the launch traced here: 73.2 us
  Pallas kernels  70 us (95%)
  local copies, waits for them, and re-layouts  2.52 us (3%)
    pallas_call x1, Pallas kernels, on_device(): pl.pallas_call(functools.partial(kernel, doms, slabs), out_shape=[jax.Sha...  70 us
    unnamed x4, local copies, waits for them, and re-layouts  2.52 us

profile of v6, /device:TPU:1, one launch (start us, length us, event | category | flops | bytes accessed | tf_op | source)
XLA Modules:
  0.0 73.2 jit_solution(17240624046029112930)
XLA Ops:
  0.6 70.0 %shard_map.104 = (f32[3,8,8,512]{3,2,1,0:T(8,128)}, f32[3,16384]{1,0:T(4,128)}) custom-call(f32[128,128]{1,0:T(8,128)} %bitcast.5, s32[576,128]{1,0:T(8,128)} %bitcast.4, s32[4,8,8,512]{3,2,1,0:T(8,128)} %shift_hbm.1, s32[4,8,8,512]{3,2,1,0:T(8,128)} %bucket_hbm.1, f32[4,8,8,512]{3,2,1,0:T(8,128)} %factor_hbm.1, f32[8,8,512]{2,1,0:T(8,128)} %rigidity.1, ...), custom_call_target="tpu_custom_call" | custom-call | tf_op jit(solution)/shard_map/pallas_call | solution.py:691
  70.6 0.0 copy-start
  70.7 1.8 %copy.13 = f32[3,8,8,512]{3,2,1,0:T(8,128)} copy(f32[3,8,8,512]{3,2,1,0:T(8,128)} %get-tuple-element.4) | data formatting | bytes 786432
  72.5 0.0 copy-done
  72.5 0.7 copy.14
Async XLA Ops:
  70.6 1.8 %copy-start = (f32[3,16384]{1,0:T(4,128)S(1)}, f32[3,16384]{1,0:T(4,128)}, u32[]{:S(2)}) copy-start(f32[3,16384]{1,0:T(4,128)} %get-tuple-element.5) | copy-start | bytes 589828
